TPU v7x, 512 devices: a whole 4x8x8 slice. The times are simulated.
512 devices in a mesh: depth: 32 (over y, x), strip: 16 (over z, core).
Axes of the slice: x: 4, y: 8, z: 8, core: 2. Of those that a mesh axis runs over, the one named last changes fastest.
Arguments:
- arrivals: float32 [32, 1, 4, 512, 128], P('depth', None, None, 'strip'), may hold values from -6 to 6
- feed: float32 [3, 1, 4, 512, 128], P(None, None, None, 'strip'), may hold values from -6 to 6
- velocity_index: int32 [64, 512, 128], P('depth', 'strip'), may hold values from 0 to 31
- offsets: int32 [16], replicated, may hold values from -8 to 8, as said below
- coef_table: float32 [35, 9, 2, 1, 32], replicated, may hold values from -1.8 to 1.8
Outputs:
- image: float32 [64, 16, 512, 128], P('depth', None, 'strip')
- outflow: float32 [32, 1, 4, 512, 128], P('depth', None, None, 'strip')
Inputs may be any that keep to these rules, and one draw needn't show every extreme that they name: The 16 offsets are distinct, and both -8 and 8 occur among them.
All inputs are finite; a program needn't handle non-finite values.
Results may differ from a plain program's by a relative error of at most 0.00025.
Values sent between devices are 32-bit elements; how exact they have to be, the bound alone decides.
A program may use at most 64 MiB of HBM per device.

v0:
```python
import jax
import jax.numpy as jnp
from jax import lax
from jax.sharding import PartitionSpec as P

LEVELS = 32
ORDER = 8


def with_halo(cells, sides, width):
    for axis, dim in sides:
        count = lax.axis_size(axis)
        ends = count - 1
        head = lax.slice_in_dim(cells, 0, width, axis=dim)
        tail = lax.slice_in_dim(cells, cells.shape[dim] - width, cells.shape[dim], axis=dim)
        cells = jnp.concatenate(
            [
                lax.ppermute(tail, axis, [(i, (i + 1) % count) for i in range(ends)]),
                cells,
                lax.ppermute(head, axis, [((i + 1) % count, i) for i in range(ends)]),
            ],
            axis=dim,
        )
    return cells


def passed_along(value, axis, steps):
    count = lax.axis_size(axis)
    initial, last = (max(0, -steps), min(count, count - steps))
    return lax.ppermute(value, axis, [(source, source + steps) for source in range(initial, last)])


def lateral(field):
    lead = [(0, 0)] * (field.ndim - 2)
    along_y = jnp.pad(field, lead + [(0, 0), (1, 1)])
    smooth_y = field + 0.5 * (along_y[..., 2:] + along_y[..., :-2])
    along_x = jnp.pad(smooth_y, lead + [(1, 1), (0, 0)])
    smooth_x = smooth_y + 0.5 * (along_x[..., 2:, :] + along_x[..., :-2, :])
    return 0.5 * smooth_x - field


def weighted(total, term, coef_re, coef_im):
    source_re = term[..., 0, :, :]
    source_im = term[..., 1, :, :]
    receiver_re = term[..., 2, :, :]
    receiver_im = term[..., 3, :, :]
    piece = jnp.stack(
        [
            coef_re * source_re - coef_im * source_im,
            coef_re * source_im + coef_im * source_re,
            coef_re * receiver_re + coef_im * receiver_im,
            coef_re * receiver_im - coef_im * receiver_re,
        ],
        axis=-3,
    )
    return total + piece


def edge_mask(strip_pos, width, total_cells, margin):
    cells = strip_pos * width - margin + jnp.arange(width + 2 * margin, dtype=jnp.int32)
    return ((cells >= 0) & (cells < total_cells)).astype(jnp.float32)[:, None]


def level_hot(levels):
    flattened = levels.reshape(1, -1)
    return (jnp.arange(LEVELS, dtype=jnp.int32).reshape(-1, 1) == flattened).astype(jnp.float32)


def coef_sets(batch_table, hot, span, lane_cells):
    flattened = jnp.dot(
        batch_table.reshape(-1, batch_table.shape[-1]),
        hot,
        precision=lax.Precision.HIGHEST,
        preferred_element_type=jnp.float32,
    )
    return flattened.reshape(batch_table.shape[0], 2, batch_table.shape[2], span, lane_cells)


def extrapolate(padded, coefficients, mask, start, count):

    def kept(values):
        return lax.slice_in_dim(values, start, start + count, axis=2)

    earlier = padded
    total = weighted(
        jnp.zeros_like(kept(padded)), kept(padded), coefficients[0, 0], coefficients[0, 1]
    )
    current = lateral(padded) * mask
    total = weighted(total, kept(current), coefficients[1, 0], coefficients[1, 1])
    for order in range(2, ORDER + 1):
        following = (2.0 * lateral(current) - earlier) * mask
        earlier, current = (current, following)
        total = weighted(total, kept(current), coefficients[order, 0], coefficients[order, 1])
    return total


def offset_image(padded, margin, offsets, width):
    rows = []
    for index in range(offsets.shape[0]):
        offset = offsets[index]
        source = lax.dynamic_slice_in_dim(padded, margin - offset, width, axis=2)
        receiver = lax.dynamic_slice_in_dim(padded, margin + offset, width, axis=2)
        rows.append(jnp.sum(source[:, 0] * receiver[:, 2] + source[:, 1] * receiver[:, 3], axis=0))
    return jnp.stack(rows, axis=0)


def per_device(arrivals, feed, velocity_index, offsets, coef_table):
    field = arrivals[0]
    width = field.shape[2]
    lane_cells = field.shape[3]
    section = lax.axis_index("depth")
    sections = lax.axis_size("depth")
    strip_pos = lax.axis_index("strip")
    total_cells = width * lax.axis_size("strip")
    layers = velocity_index.shape[0]
    ticks = feed.shape[0] + 1
    image = jnp.zeros((layers, offsets.shape[0], width, lane_cells), jnp.float32)
    level_hots = [level_hot(velocity_index[row]) for row in range(layers)]
    mask = edge_mask(strip_pos, width, total_cells, ORDER)
    for tick in range(ticks):
        batch_table = lax.dynamic_index_in_dim(
            coef_table, tick - section + sections - 1, 0, keepdims=False
        )
        for row in range(layers):
            padded = with_halo(field, (("strip", 2),), ORDER)
            if row > 0:
                image = image.at[row - 1].add(offset_image(padded, ORDER, offsets, width))
            coefficients = coef_sets(batch_table, level_hots[row], width, lane_cells)
            field = extrapolate(padded, coefficients, mask, ORDER, width)
        padded = with_halo(field, (("strip", 2),), ORDER)
        image = image.at[layers - 1].add(offset_image(padded, ORDER, offsets, width))
        if tick + 1 < ticks:
            moved = passed_along(field, "depth", 1)
            field = jnp.where(section == 0, feed[tick], moved)
    return (image, field[None])


def solution(mesh):
    placed = (
        P("depth", None, None, "strip", None),
        P(None, None, None, "strip", None),
        P("depth", "strip", None),
        P(),
        P(),
    )
    return jax.shard_map(
        per_device,
        mesh=mesh,
        in_specs=placed,
        out_specs=(P("depth", None, "strip", None), P("depth", None, None, "strip", None)),
        check_vma=False,
    )
```

profile of v0, /device:TPU:223, one launch (start us, length us, event | category | flops | bytes accessed | tf_op | source)
XLA Modules:
  0.0 192.8 jit_solution(10380294880644212521)
XLA Ops:
  2.0 2.6 %collective-permute-start.1 = (f32[1,4,8,128]{3,2,1,0:T(8,128)}, f32[1,4,8,128]{3,2,1,0:T(8,128)S(1)}, u32[]{:S(2)}, u32[]{:S(2)}) collective-permute-start(f32[1,4,8,128]{3,2,1,0:T(8,128)} %get-tuple-element.463), channel_id=1, source_target_pairs={{1,0},{2,1},{3,2},{4,3},{5,4},{6,5},{7,6},{8,7},{9,8},{10,9},{11,1... | collective-permute-start | bytes 49160 | tf_op jit(solution)/shard_map/ppermute | solution.py:20
  4.6 5.1 %collective-permute-start = (f32[1,4,8,128]{3,2,1,0:T(8,128)}, f32[1,4,8,128]{3,2,1,0:T(8,128)S(1)}, u32[]{:S(2)}, u32[]{:S(2)}) collective-permute-start(f32[1,4,8,128]{3,2,1,0:T(8,128)} %get-tuple-element.462), channel_id=1, source_target_pairs={{0,1},{1,2},{2,3},{3,4},{4,5},{5,6},{6,7},{7,8},{8,9},{9,10},{10,1... | collective-permute-start | bytes 49160 | tf_op jit(solution)/shard_map/ppermute | solution.py:18
  9.7 2.0 %constant_dynamic-slice_fusion.320 = (f32[1,9,2,1,32]{0,4,3,2,1:T(8,128)S(1)}, f32[1,9,2,1,32]{0,4,3,2,1:T(8,128)S(1)}, f32[1,9,2,1,32]{0,4,3,2,1:T(8,128)S(1)}, f32[1,9,2,1,32]{0,4,3,2,1:T(8,128)S(1)}) fusion(f32[35,9,2,1,32]{0,4,3,2,1:T(8,128)} %param.25, s32[]{:T(128)S(6)} %select_n.131, s32[]{:T(128)S(6)} %select_n.126, s32[]{:T(128)S(6)} %select_n.93, ...), kind=kLoop, calls=%fused_computation.633 | loop fusion | bytes 18448 | tf_op jit(solution)/shard_map/jit(dynamic_index_in_dim)/dynamic_slice | solution.py:121
  72.8 2.1 %collective-permute-start.3 = (f32[1,4,8,128]{3,2,1,0:T(8,128)S(1)}, f32[1,4,8,128]{3,2,1,0:T(8,128)S(1)}, u32[]{:S(2)}, u32[]{:S(2)}) collective-permute-start(f32[1,4,8,128]{3,2,1,0:T(8,128)S(1)} %get-tuple-element.461), channel_id=1, source_target_pairs={{1,0},{2,1},{3,2},{4,3},{5,4},{6,5},{7,6},{8,7},{9,8},{10,9},{11,1... | collective-permute-start | bytes 49160 | tf_op jit(solution)/shard_map/ppermute | solution.py:20
  74.8 4.9 %collective-permute-start.2 = (f32[1,4,8,128]{3,2,1,0:T(8,128)S(1)}, f32[1,4,8,128]{3,2,1,0:T(8,128)S(1)}, u32[]{:S(2)}, u32[]{:S(2)}) collective-permute-start(f32[1,4,8,128]{3,2,1,0:T(8,128)S(1)} %get-tuple-element.460), channel_id=1, source_target_pairs={{0,1},{1,2},{2,3},{3,4},{4,5},{5,6},{6,7},{7,8},{8,9},{9,10},{10,1... | collective-permute-start | bytes 49160 | tf_op jit(solution)/shard_map/ppermute | solution.py:18
  82.4 4.3 %collective-permute-start.6 = (f32[1,4,32,128]{3,2,1,0:T(8,128)S(1)}, f32[1,4,32,128]{3,2,1,0:T(8,128)S(1)}, u32[]{:S(2)}, u32[]{:S(2)}) collective-permute-start(f32[1,4,32,128]{3,2,1,0:T(8,128)S(1)} %fusion.723), channel_id=1, source_target_pairs={{0,16},{16,32},{32,48},{48,64},{64,80},{80,96},{96,112},{112,128},... | collective-permute-start | bytes 196616 | tf_op jit(solution)/shard_map/ppermute | solution.py:30
  86.7 1.9 collective-permute-start.5
  88.6 5.7 %collective-permute-start.4 = (f32[1,4,8,128]{3,2,1,0:T(8,128)S(1)}, f32[1,4,8,128]{3,2,1,0:T(8,128)S(1)}, u32[]{:S(2)}, u32[]{:S(2)}) collective-permute-start(f32[1,4,8,128]{3,2,1,0:T(8,128)S(1)} %get-tuple-element.458), channel_id=1, source_target_pairs={{0,1},{1,2},{2,3},{3,4},{4,5},{5,6},{6,7},{7,8},{8,9},{9,10},{10,1... | collective-permute-start | bytes 49160 | tf_op jit(solution)/shard_map/ppermute | solution.py:18
  96.7 1.9 collective-permute-start.8
  98.6 5.4 %collective-permute-start.7 = (f32[1,4,8,128]{3,2,1,0:T(8,128)S(1)}, f32[1,4,8,128]{3,2,1,0:T(8,128)S(1)}, u32[]{:S(2)}, u32[]{:S(2)}) collective-permute-start(f32[1,4,8,128]{3,2,1,0:T(8,128)S(1)} %get-tuple-element.456), channel_id=1, source_target_pairs={{0,1},{1,2},{2,3},{3,4},{4,5},{5,6},{6,7},{7,8},{8,9},{9,10},{10,1... | collective-permute-start | bytes 49160 | tf_op jit(solution)/shard_map/ppermute | solution.py:18
  106.7 1.9 collective-permute-start.10
  108.7 5.6 %collective-permute-start.9 = (f32[1,4,8,128]{3,2,1,0:T(8,128)S(1)}, f32[1,4,8,128]{3,2,1,0:T(8,128)S(1)}, u32[]{:S(2)}, u32[]{:S(2)}) collective-permute-start(f32[1,4,8,128]{3,2,1,0:T(8,128)S(1)} %get-tuple-element.454), channel_id=1, source_target_pairs={{0,1},{1,2},{2,3},{3,4},{4,5},{5,6},{6,7},{7,8},{8,9},{9,10},{10,1... | collective-permute-start | bytes 49160 | tf_op jit(solution)/shard_map/ppermute | solution.py:18
  116.8 3.1 %collective-permute-start.13 = (f32[1,4,32,128]{3,2,1,0:T(8,128)S(1)}, f32[1,4,32,128]{3,2,1,0:T(8,128)S(1)}, u32[]{:S(2)}, u32[]{:S(2)}) collective-permute-start(f32[1,4,32,128]{3,2,1,0:T(8,128)S(1)} %fusion.737), channel_id=1, source_target_pairs={{0,16},{16,32},{32,48},{48,64},{64,80},{80,96},{96,112},{112,128},... | collective-permute-start | bytes 196616 | tf_op jit(solution)/shard_map/ppermute | solution.py:30
  120.5 1.9 collective-permute-start.12
  122.4 5.7 %collective-permute-start.11 = (f32[1,4,8,128]{3,2,1,0:T(8,128)S(1)}, f32[1,4,8,128]{3,2,1,0:T(8,128)S(1)}, u32[]{:S(2)}, u32[]{:S(2)}) collective-permute-start(f32[1,4,8,128]{3,2,1,0:T(8,128)S(1)} %get-tuple-element.452), channel_id=1, source_target_pairs={{0,1},{1,2},{2,3},{3,4},{4,5},{5,6},{6,7},{7,8},{8,9},{9,10},{10,1... | collective-permute-start | bytes 49160 | tf_op jit(solution)/shard_map/ppermute | solution.py:18
  129.6 1.9 collective-permute-start.15
  131.6 5.4 %collective-permute-start.14 = (f32[1,4,8,128]{3,2,1,0:T(8,128)S(1)}, f32[1,4,8,128]{3,2,1,0:T(8,128)S(1)}, u32[]{:S(2)}, u32[]{:S(2)}) collective-permute-start(f32[1,4,8,128]{3,2,1,0:T(8,128)S(1)} %get-tuple-element.450), channel_id=1, source_target_pairs={{0,1},{1,2},{2,3},{3,4},{4,5},{5,6},{6,7},{7,8},{8,9},{9,10},{10,1... | collective-permute-start | bytes 49160 | tf_op jit(solution)/shard_map/ppermute | solution.py:18
  139.7 1.9 collective-permute-start.17
  141.6 5.4 %collective-permute-start.16 = (f32[1,4,8,128]{3,2,1,0:T(8,128)S(1)}, f32[1,4,8,128]{3,2,1,0:T(8,128)S(1)}, u32[]{:S(2)}, u32[]{:S(2)}) collective-permute-start(f32[1,4,8,128]{3,2,1,0:T(8,128)S(1)} %get-tuple-element.448), channel_id=1, source_target_pairs={{0,1},{1,2},{2,3},{3,4},{4,5},{5,6},{6,7},{7,8},{8,9},{9,10},{10,1... | collective-permute-start | bytes 49160 | tf_op jit(solution)/shard_map/ppermute | solution.py:18
  149.7 3.1 %collective-permute-start.20 = (f32[1,4,32,128]{3,2,1,0:T(8,128)S(1)}, f32[1,4,32,128]{3,2,1,0:T(8,128)S(1)}, u32[]{:S(2)}, u32[]{:S(2)}) collective-permute-start(f32[1,4,32,128]{3,2,1,0:T(8,128)S(1)} %fusion.751), channel_id=1, source_target_pairs={{0,16},{16,32},{32,48},{48,64},{64,80},{80,96},{96,112},{112,128},... | collective-permute-start | bytes 196616 | tf_op jit(solution)/shard_map/ppermute | solution.py:30
  155.3 5.7 %collective-permute-start.18 = (f32[1,4,8,128]{3,2,1,0:T(8,128)S(1)}, f32[1,4,8,128]{3,2,1,0:T(8,128)S(1)}, u32[]{:S(2)}, u32[]{:S(2)}) collective-permute-start(f32[1,4,8,128]{3,2,1,0:T(8,128)S(1)} %get-tuple-element.446), channel_id=1, source_target_pairs={{0,1},{1,2},{2,3},{3,4},{4,5},{5,6},{6,7},{7,8},{8,9},{9,10},{10,1... | collective-permute-start | bytes 49160 | tf_op jit(solution)/shard_map/ppermute | solution.py:18
  164.5 5.4 %collective-permute-start.21 = (f32[1,4,8,128]{3,2,1,0:T(8,128)S(1)}, f32[1,4,8,128]{3,2,1,0:T(8,128)S(1)}, u32[]{:S(2)}, u32[]{:S(2)}) collective-permute-start(f32[1,4,8,128]{3,2,1,0:T(8,128)S(1)} %get-tuple-element.444), channel_id=1, source_target_pairs={{0,1},{1,2},{2,3},{3,4},{4,5},{5,6},{6,7},{7,8},{8,9},{9,10},{10,1... | collective-permute-start | bytes 49160 | tf_op jit(solution)/shard_map/ppermute | solution.py:18
  174.5 5.4 %collective-permute-start.23 = (f32[1,4,8,128]{3,2,1,0:T(8,128)S(1)}, f32[1,4,8,128]{3,2,1,0:T(8,128)S(1)}, u32[]{:S(2)}, u32[]{:S(2)}) collective-permute-start(f32[1,4,8,128]{3,2,1,0:T(8,128)S(1)} %get-tuple-element.442), channel_id=1, source_target_pairs={{0,1},{1,2},{2,3},{3,4},{4,5},{5,6},{6,7},{7,8},{8,9},{9,10},{10,1... | collective-permute-start | bytes 49160 | tf_op jit(solution)/shard_map/ppermute | solution.py:18
  185.1 5.4 %collective-permute-start.25 = (f32[1,4,8,128]{3,2,1,0:T(8,128)S(1)}, f32[1,4,8,128]{3,2,1,0:T(8,128)S(1)}, u32[]{:S(2)}, u32[]{:S(2)}) collective-permute-start(f32[1,4,8,128]{3,2,1,0:T(8,128)S(1)} %get-tuple-element.440), channel_id=1, source_target_pairs={{0,1},{1,2},{2,3},{3,4},{4,5},{5,6},{6,7},{7,8},{8,9},{9,10},{10,1... | collective-permute-start | bytes 49160 | tf_op jit(solution)/shard_map/ppermute | solution.py:18
  (500 shorter events, 55.7 us)
Async XLA Ops:
  2.0 62.5 %collective-permute-start.1 = (f32[1,4,8,128]{3,2,1,0:T(8,128)}, f32[1,4,8,128]{3,2,1,0:T(8,128)S(1)}, u32[]{:S(2)}, u32[]{:S(2)}) collective-permute-start(f32[1,4,8,128]{3,2,1,0:T(8,128)} %get-tuple-element.463), channel_id=1, source_target_pairs={{1,0},{2,1},{3,2},{4,3},{5,4},{6,5},{7,6},{8,7},{9,8},{10,9},{11,1... | collective-permute-start | bytes 49160 | tf_op jit(solution)/shard_map/ppermute | solution.py:20
  4.6 59.9 %collective-permute-start = (f32[1,4,8,128]{3,2,1,0:T(8,128)}, f32[1,4,8,128]{3,2,1,0:T(8,128)S(1)}, u32[]{:S(2)}, u32[]{:S(2)}) collective-permute-start(f32[1,4,8,128]{3,2,1,0:T(8,128)} %get-tuple-element.462), channel_id=1, source_target_pairs={{0,1},{1,2},{2,3},{3,4},{4,5},{5,6},{6,7},{7,8},{8,9},{9,10},{10,1... | collective-permute-start | bytes 49160 | tf_op jit(solution)/shard_map/ppermute | solution.py:18
  72.8 7.0 %collective-permute-start.3 = (f32[1,4,8,128]{3,2,1,0:T(8,128)S(1)}, f32[1,4,8,128]{3,2,1,0:T(8,128)S(1)}, u32[]{:S(2)}, u32[]{:S(2)}) collective-permute-start(f32[1,4,8,128]{3,2,1,0:T(8,128)S(1)} %get-tuple-element.461), channel_id=1, source_target_pairs={{1,0},{2,1},{3,2},{4,3},{5,4},{6,5},{7,6},{8,7},{9,8},{10,9},{11,1... | collective-permute-start | bytes 49160 | tf_op jit(solution)/shard_map/ppermute | solution.py:20
  82.4 13.4 %collective-permute-start.6 = (f32[1,4,32,128]{3,2,1,0:T(8,128)S(1)}, f32[1,4,32,128]{3,2,1,0:T(8,128)S(1)}, u32[]{:S(2)}, u32[]{:S(2)}) collective-permute-start(f32[1,4,32,128]{3,2,1,0:T(8,128)S(1)} %fusion.723), channel_id=1, source_target_pairs={{0,16},{16,32},{32,48},{48,64},{64,80},{80,96},{96,112},{112,128},... | collective-permute-start | bytes 196616 | tf_op jit(solution)/shard_map/ppermute | solution.py:30
  86.7 8.4 %collective-permute-start.5 = (f32[1,4,8,128]{3,2,1,0:T(8,128)S(1)}, f32[1,4,8,128]{3,2,1,0:T(8,128)S(1)}, u32[]{:S(2)}, u32[]{:S(2)}) collective-permute-start(f32[1,4,8,128]{3,2,1,0:T(8,128)S(1)} %get-tuple-element.459), channel_id=1, source_target_pairs={{1,0},{2,1},{3,2},{4,3},{5,4},{6,5},{7,6},{8,7},{9,8},{10,9},{11,1... | collective-permute-start | bytes 49160 | tf_op jit(solution)/shard_map/ppermute | solution.py:20
  88.6 6.6 %collective-permute-start.4 = (f32[1,4,8,128]{3,2,1,0:T(8,128)S(1)}, f32[1,4,8,128]{3,2,1,0:T(8,128)S(1)}, u32[]{:S(2)}, u32[]{:S(2)}) collective-permute-start(f32[1,4,8,128]{3,2,1,0:T(8,128)S(1)} %get-tuple-element.458), channel_id=1, source_target_pairs={{0,1},{1,2},{2,3},{3,4},{4,5},{5,6},{6,7},{7,8},{8,9},{9,10},{10,1... | collective-permute-start | bytes 49160 | tf_op jit(solution)/shard_map/ppermute | solution.py:18
  96.7 7.4 %collective-permute-start.8 = (f32[1,4,8,128]{3,2,1,0:T(8,128)S(1)}, f32[1,4,8,128]{3,2,1,0:T(8,128)S(1)}, u32[]{:S(2)}, u32[]{:S(2)}) collective-permute-start(f32[1,4,8,128]{3,2,1,0:T(8,128)S(1)} %get-tuple-element.457), channel_id=1, source_target_pairs={{1,0},{2,1},{3,2},{4,3},{5,4},{6,5},{7,6},{8,7},{9,8},{10,9},{11,1... | collective-permute-start | bytes 49160 | tf_op jit(solution)/shard_map/ppermute | solution.py:20
  98.6 6.3 %collective-permute-start.7 = (f32[1,4,8,128]{3,2,1,0:T(8,128)S(1)}, f32[1,4,8,128]{3,2,1,0:T(8,128)S(1)}, u32[]{:S(2)}, u32[]{:S(2)}) collective-permute-start(f32[1,4,8,128]{3,2,1,0:T(8,128)S(1)} %get-tuple-element.456), channel_id=1, source_target_pairs={{0,1},{1,2},{2,3},{3,4},{4,5},{5,6},{6,7},{7,8},{8,9},{9,10},{10,1... | collective-permute-start | bytes 49160 | tf_op jit(solution)/shard_map/ppermute | solution.py:18
  106.7 7.6 %collective-permute-start.10 = (f32[1,4,8,128]{3,2,1,0:T(8,128)S(1)}, f32[1,4,8,128]{3,2,1,0:T(8,128)S(1)}, u32[]{:S(2)}, u32[]{:S(2)}) collective-permute-start(f32[1,4,8,128]{3,2,1,0:T(8,128)S(1)} %get-tuple-element.455), channel_id=1, source_target_pairs={{1,0},{2,1},{3,2},{4,3},{5,4},{6,5},{7,6},{8,7},{9,8},{10,9},{11,1... | collective-permute-start | bytes 49160 | tf_op jit(solution)/shard_map/ppermute | solution.py:20
  108.7 6.3 %collective-permute-start.9 = (f32[1,4,8,128]{3,2,1,0:T(8,128)S(1)}, f32[1,4,8,128]{3,2,1,0:T(8,128)S(1)}, u32[]{:S(2)}, u32[]{:S(2)}) collective-permute-start(f32[1,4,8,128]{3,2,1,0:T(8,128)S(1)} %get-tuple-element.454), channel_id=1, source_target_pairs={{0,1},{1,2},{2,3},{3,4},{4,5},{5,6},{6,7},{7,8},{8,9},{9,10},{10,1... | collective-permute-start | bytes 49160 | tf_op jit(solution)/shard_map/ppermute | solution.py:18
  116.8 12.8 %collective-permute-start.13 = (f32[1,4,32,128]{3,2,1,0:T(8,128)S(1)}, f32[1,4,32,128]{3,2,1,0:T(8,128)S(1)}, u32[]{:S(2)}, u32[]{:S(2)}) collective-permute-start(f32[1,4,32,128]{3,2,1,0:T(8,128)S(1)} %fusion.737), channel_id=1, source_target_pairs={{0,16},{16,32},{32,48},{48,64},{64,80},{80,96},{96,112},{112,128},... | collective-permute-start | bytes 196616 | tf_op jit(solution)/shard_map/ppermute | solution.py:30
  120.5 7.7 %collective-permute-start.12 = (f32[1,4,8,128]{3,2,1,0:T(8,128)S(1)}, f32[1,4,8,128]{3,2,1,0:T(8,128)S(1)}, u32[]{:S(2)}, u32[]{:S(2)}) collective-permute-start(f32[1,4,8,128]{3,2,1,0:T(8,128)S(1)} %get-tuple-element.453), channel_id=1, source_target_pairs={{1,0},{2,1},{3,2},{4,3},{5,4},{6,5},{7,6},{8,7},{9,8},{10,9},{11,1... | collective-permute-start | bytes 49160 | tf_op jit(solution)/shard_map/ppermute | solution.py:20
  122.4 6.6 %collective-permute-start.11 = (f32[1,4,8,128]{3,2,1,0:T(8,128)S(1)}, f32[1,4,8,128]{3,2,1,0:T(8,128)S(1)}, u32[]{:S(2)}, u32[]{:S(2)}) collective-permute-start(f32[1,4,8,128]{3,2,1,0:T(8,128)S(1)} %get-tuple-element.452), channel_id=1, source_target_pairs={{0,1},{1,2},{2,3},{3,4},{4,5},{5,6},{6,7},{7,8},{8,9},{9,10},{10,1... | collective-permute-start | bytes 49160 | tf_op jit(solution)/shard_map/ppermute | solution.py:18
  129.6 7.4 %collective-permute-start.15 = (f32[1,4,8,128]{3,2,1,0:T(8,128)S(1)}, f32[1,4,8,128]{3,2,1,0:T(8,128)S(1)}, u32[]{:S(2)}, u32[]{:S(2)}) collective-permute-start(f32[1,4,8,128]{3,2,1,0:T(8,128)S(1)} %get-tuple-element.451), channel_id=1, source_target_pairs={{1,0},{2,1},{3,2},{4,3},{5,4},{6,5},{7,6},{8,7},{9,8},{10,9},{11,1... | collective-permute-start | bytes 49160 | tf_op jit(solution)/shard_map/ppermute | solution.py:20
  131.6 6.3 %collective-permute-start.14 = (f32[1,4,8,128]{3,2,1,0:T(8,128)S(1)}, f32[1,4,8,128]{3,2,1,0:T(8,128)S(1)}, u32[]{:S(2)}, u32[]{:S(2)}) collective-permute-start(f32[1,4,8,128]{3,2,1,0:T(8,128)S(1)} %get-tuple-element.450), channel_id=1, source_target_pairs={{0,1},{1,2},{2,3},{3,4},{4,5},{5,6},{6,7},{7,8},{8,9},{9,10},{10,1... | collective-permute-start | bytes 49160 | tf_op jit(solution)/shard_map/ppermute | solution.py:18
  139.7 7.4 %collective-permute-start.17 = (f32[1,4,8,128]{3,2,1,0:T(8,128)S(1)}, f32[1,4,8,128]{3,2,1,0:T(8,128)S(1)}, u32[]{:S(2)}, u32[]{:S(2)}) collective-permute-start(f32[1,4,8,128]{3,2,1,0:T(8,128)S(1)} %get-tuple-element.449), channel_id=1, source_target_pairs={{1,0},{2,1},{3,2},{4,3},{5,4},{6,5},{7,6},{8,7},{9,8},{10,9},{11,1... | collective-permute-start | bytes 49160 | tf_op jit(solution)/shard_map/ppermute | solution.py:20
  149.7 12.8 %collective-permute-start.20 = (f32[1,4,32,128]{3,2,1,0:T(8,128)S(1)}, f32[1,4,32,128]{3,2,1,0:T(8,128)S(1)}, u32[]{:S(2)}, u32[]{:S(2)}) collective-permute-start(f32[1,4,32,128]{3,2,1,0:T(8,128)S(1)} %fusion.751), channel_id=1, source_target_pairs={{0,16},{16,32},{32,48},{48,64},{64,80},{80,96},{96,112},{112,128},... | collective-permute-start | bytes 196616 | tf_op jit(solution)/shard_map/ppermute | solution.py:30
  153.4 7.7 %collective-permute-start.19 = (f32[1,4,8,128]{3,2,1,0:T(8,128)S(1)}, f32[1,4,8,128]{3,2,1,0:T(8,128)S(1)}, u32[]{:S(2)}, u32[]{:S(2)}) collective-permute-start(f32[1,4,8,128]{3,2,1,0:T(8,128)S(1)} %get-tuple-element.447), channel_id=1, source_target_pairs={{1,0},{2,1},{3,2},{4,3},{5,4},{6,5},{7,6},{8,7},{9,8},{10,9},{11,1... | collective-permute-start | bytes 49160 | tf_op jit(solution)/shard_map/ppermute | solution.py:20
  155.3 6.6 %collective-permute-start.18 = (f32[1,4,8,128]{3,2,1,0:T(8,128)S(1)}, f32[1,4,8,128]{3,2,1,0:T(8,128)S(1)}, u32[]{:S(2)}, u32[]{:S(2)}) collective-permute-start(f32[1,4,8,128]{3,2,1,0:T(8,128)S(1)} %get-tuple-element.446), channel_id=1, source_target_pairs={{0,1},{1,2},{2,3},{3,4},{4,5},{5,6},{6,7},{7,8},{8,9},{9,10},{10,1... | collective-permute-start | bytes 49160 | tf_op jit(solution)/shard_map/ppermute | solution.py:18
  162.5 7.4 %collective-permute-start.22 = (f32[1,4,8,128]{3,2,1,0:T(8,128)S(1)}, f32[1,4,8,128]{3,2,1,0:T(8,128)S(1)}, u32[]{:S(2)}, u32[]{:S(2)}) collective-permute-start(f32[1,4,8,128]{3,2,1,0:T(8,128)S(1)} %get-tuple-element.445), channel_id=1, source_target_pairs={{1,0},{2,1},{3,2},{4,3},{5,4},{6,5},{7,6},{8,7},{9,8},{10,9},{11,1... | collective-permute-start | bytes 49160 | tf_op jit(solution)/shard_map/ppermute | solution.py:20
  164.5 6.3 %collective-permute-start.21 = (f32[1,4,8,128]{3,2,1,0:T(8,128)S(1)}, f32[1,4,8,128]{3,2,1,0:T(8,128)S(1)}, u32[]{:S(2)}, u32[]{:S(2)}) collective-permute-start(f32[1,4,8,128]{3,2,1,0:T(8,128)S(1)} %get-tuple-element.444), channel_id=1, source_target_pairs={{0,1},{1,2},{2,3},{3,4},{4,5},{5,6},{6,7},{7,8},{8,9},{9,10},{10,1... | collective-permute-start | bytes 49160 | tf_op jit(solution)/shard_map/ppermute | solution.py:18
  172.6 7.4 %collective-permute-start.24 = (f32[1,4,8,128]{3,2,1,0:T(8,128)S(1)}, f32[1,4,8,128]{3,2,1,0:T(8,128)S(1)}, u32[]{:S(2)}, u32[]{:S(2)}) collective-permute-start(f32[1,4,8,128]{3,2,1,0:T(8,128)S(1)} %get-tuple-element.443), channel_id=1, source_target_pairs={{1,0},{2,1},{3,2},{4,3},{5,4},{6,5},{7,6},{8,7},{9,8},{10,9},{11,1... | collective-permute-start | bytes 49160 | tf_op jit(solution)/shard_map/ppermute | solution.py:20
  183.2 8.2 %collective-permute-start.26 = (f32[1,4,8,128]{3,2,1,0:T(8,128)S(1)}, f32[1,4,8,128]{3,2,1,0:T(8,128)S(1)}, u32[]{:S(2)}, u32[]{:S(2)}) collective-permute-start(f32[1,4,8,128]{3,2,1,0:T(8,128)S(1)} %get-tuple-element.441), channel_id=1, source_target_pairs={{1,0},{2,1},{3,2},{4,3},{5,4},{6,5},{7,6},{8,7},{9,8},{10,9},{11,1... | collective-permute-start | bytes 49160 | tf_op jit(solution)/shard_map/ppermute | solution.py:20
  185.1 6.3 %collective-permute-start.25 = (f32[1,4,8,128]{3,2,1,0:T(8,128)S(1)}, f32[1,4,8,128]{3,2,1,0:T(8,128)S(1)}, u32[]{:S(2)}, u32[]{:S(2)}) collective-permute-start(f32[1,4,8,128]{3,2,1,0:T(8,128)S(1)} %get-tuple-element.440), channel_id=1, source_target_pairs={{0,1},{1,2},{2,3},{3,4},{4,5},{5,6},{6,7},{7,8},{8,9},{9,10},{10,1... | collective-permute-start | bytes 49160 | tf_op jit(solution)/shard_map/ppermute | solution.py:18
  (32 other events, 70.4 us)
where the time goes:
time: 196 us; the launch traced here: 193 us
  starting transfers between devices  99.6 us (51%)
  between operations  43.2 us (22%)
  other arithmetic  19.4 us (10%)
  local copies, waits for them, and re-layouts  18.9 us (10%)
  waiting for transfers between devices  7.2 us (4%)
  matrix products  4.48 us (2%)
    ppermute x12, starting transfers between devices, with_halo(): lax.ppermute(tail, axis, [(i, (i + 1) % count) for i in range(ends)])  65.2 us
    ppermute x12, starting transfers between devices, with_halo(): lax.ppermute(head, axis, [((i + 1) % count, i) for i in range(ends)])  23.8 us
    ppermute x3, starting transfers between devices, passed_along(): lax.ppermute(value, axis, [(source, source + steps) for source in range(i...  10.6 us
    unnamed x73, local copies, waits for them, and re-layouts  9.09 us
    add x64, other arithmetic, lateral(): smooth_y = field + 0.5 * (along_y[..., 2:] + along_y[..., :-2])  7.42 us
    ppermute x12, waiting for transfers between devices, with_halo(): lax.ppermute(tail, axis, [(i, (i + 1) % count) for i in range(ends)])  7.16 us
    dot_general x8, matrix products, coef_sets(): jnp.dot(batch_table.reshape(-1, batch_table.shape[-1]), hot, precision=la...  4.48 us
    mul x56, other arithmetic, extrapolate(): following = (2.0 * lateral(current) - earlier) * mask  4.38 us
  transfers between devices with their start and end apart: 27, of which 10 were waited for; matrix products, arithmetic and copies ran while one was open for 9% of the time, Pallas kernels for 0%

commit v1 on v0

v1 whole, which is shorter than its diff:
```python
import functools

import jax
import jax.numpy as jnp
from jax import lax
from jax.experimental import pallas as pl
from jax.experimental.pallas import tpu as pltpu
from jax.sharding import PartitionSpec as P

MESH = pl.DeviceIdType.MESH
ORDER = 8
W = 32
NY = 128
F32 = jnp.float32

ROWS = (128, 112, 96, 80, 64, 48)
LAST = (80, 64)

MSGS = {}
for _s in (1, -1, 2, -2):
    MSGS["a", _s] = (0, _s)
    MSGS["v0", _s] = (0, _s)
for _s in (0, 1, -1):
    MSGS["v1", _s] = (-1, _s)
    MSGS["v2", _s] = (-2, _s)
    MSGS["m", _s] = (3, _s)
for _s in (1, -1):
    MSGS["f1", _s] = (0, _s)
    MSGS["f2", _s] = (0, _s)
    MSGS["i2", 1, _s] = (2, _s)
for _l in (0, 1):
    MSGS["i1", _l, 0] = (1, 0)
    MSGS["i2", _l, 0] = (2, 0)
INDEX = {name: i for i, name in enumerate(MSGS)}
PEERS = sorted(set(MSGS.values()))


def layer(rows, load, lev, tab, top, total, out):
    nb = rows // 8
    lanes = lax.broadcasted_iota(jnp.int32, (8, NY), 1)
    first, final = lanes == 0, lanes == NY - 1
    blocks = lax.broadcasted_iota(jnp.int32, (8, NY), 0) * nb + top
    inside = [(blocks + j >= 0) & (blocks + j < total) for j in range(nb)]
    quarter = [jnp.where(inside[j], 0.25, 0.0) for j in range(nb)]
    comps = range(4)
    t = [[jnp.where(inside[j], load(c, j, nb), 0.0) for j in range(nb)] for c in comps]
    hist = [t]
    p = None
    for n in range(1, ORDER + 1):
        new_t, new_p = [], []
        for c in comps:
            u = t[c]
            up = pltpu.roll(u[nb - 1], 1, 0)
            down = pltpu.roll(u[0], 7, 0)
            s = [u[j] + u[j + 1] for j in range(nb - 1)]
            tl, ql = [], []
            for j in range(nb):
                a = s[j - 1] if j else up + u[0]
                b = s[j] if j + 1 < nb else u[nb - 1] + down
                v = a + b
                sides = jnp.where(first, 0.0, pltpu.roll(v, 1, 1)) + jnp.where(
                    final, 0.0, pltpu.roll(v, NY - 1, 1)
                )
                q = (v + v) + sides
                if n == 1:
                    r = q * (quarter[j] * 0.5)
                else:
                    r = q * quarter[j] - p[c][j]
                ql.append(r)
                tl.append(r - u[j])
            new_t.append(tl)
            new_p.append(ql)
        t, p = new_t, new_p
        hist.append(t)
    for j in range(nb):
        idx = lev(j, nb)
        acc = [None] * 4
        for n in range(ORDER + 1):
            cr = jnp.take_along_axis(tab[2 * n], idx, axis=1)
            ci = jnp.take_along_axis(tab[2 * n + 1], idx, axis=1)
            sr, si, rr, ri = [hist[n][c][j] for c in comps]
            new = [
                cr * sr - ci * si,
                cr * si + ci * sr,
                cr * rr + ci * ri,
                cr * ri - ci * rr,
            ]
            acc = [new[c] if n == 0 else acc[c] + new[c] for c in comps]
        for c in comps:
            out(c, j, nb, acc[c])


def kernel(depths, strips, arr, vel, offs, feed, table, img, outflow, A, V0, V1, V2, Y0, Y1, Y2, Y3, Y4, Y5, Y6, Y7, M, I1, I2, TB, TW, ssem, rsem, lsem, tsem):
    d = lax.axis_index("depth")
    s = lax.axis_index("strip")

    def peer(shift):
        return (
            lax.rem(d + shift[0] + depths, depths),
            lax.rem(s + shift[1] + strips, strips),
        )

    barrier = pltpu.get_barrier_semaphore()
    for shift in PEERS:
        pl.semaphore_signal(barrier, inc=1, device_id=peer((-shift[0], -shift[1])), device_id_type=MESH)

    wraps = [d + k >= depths for k in range(3)]
    tick_row = [jnp.where(wraps[k], 2 * depths - 1 - d, depths - 1 - d) for k in range(3)] + [depths + 2 - d]
    tabs = [pltpu.make_async_copy(table.at[tick_row[k]], TB.at[k], tsem.at[k]) for k in range(4)]
    for copy in tabs:
        copy.start()

    def send(name, src, dst):
        i = INDEX[name]
        return pltpu.make_async_remote_copy(
            src_ref=src, dst_ref=dst, send_sem=ssem.at[i], recv_sem=rsem.at[i],
            device_id=peer(MSGS[name]), device_id_type=MESH,
        )

    def rows(ref, start, count, lead=()):
        return ref.at[(*lead, slice(None), pl.ds(start, count), slice(None))]

    own = arr.at[0, 0]
    lead1, lead2 = A.shape[1] // 2 - W // 2, V2.shape[1] // 2 - W // 2
    sends = {}
    sends["v0", 1] = (vel, rows(V0, 16, 32))
    sends["v0", -1] = (vel, rows(V0, 80, 32))
    sends["v0", 2] = (rows(vel, 16, 16), rows(V0, 0, 16))
    sends["v0", -2] = (rows(vel, 0, 16), rows(V0, 112, 16))
    sends["a", 1] = (own, rows(A, 16, 32))
    sends["a", -1] = (own, rows(A, 80, 32))
    sends["a", 2] = (rows(arr, 16, 16, (0, 0)), rows(A, 0, 16))
    sends["a", -2] = (rows(arr, 0, 16, (0, 0)), rows(A, 112, 16))
    sends["v1", 0] = (vel, rows(V1, 32, 32))
    sends["v1", 1] = (vel, rows(V1, 0, 32))
    sends["v1", -1] = (vel, rows(V1, 64, 32))
    sends["v2", 0] = (vel, rows(V2, 16, 32))
    sends["v2", 1] = (rows(vel, 16, 16), rows(V2, 0, 16))
    sends["v2", -1] = (rows(vel, 0, 16), rows(V2, 48, 16))
    for layer_ in (0, 1):
        sends["i1", layer_, 0] = (rows((Y2, Y3)[layer_], (24, 16)[layer_], 48, () if layer_ == 0 else (0,)), I1.at[layer_])
    sends["i2", 0, 0] = (rows(Y4, 8, 48), I2.at[0])
    sends["i2", 1, 0] = (rows(Y5, 8, 32), rows(I2, 8, 32, (1,)))
    sends["i2", 1, 1] = (rows(Y5, 32, 8), rows(I2, 0, 8, (1,)))
    sends["i2", 1, -1] = (rows(Y5, 8, 8), rows(I2, 40, 8, (1,)))
    moved = {0: (8, 32, 24), 1: (16, 24, 0), -1: (8, 24, 56)}
    for shift, (start, count, to) in moved.items():
        sends["m", shift] = (rows(Y5, start, count), rows(M, to, count))
    for shift, to in ((1, 8), (-1, 72)):
        sends["f1", shift] = (feed.at[0, 0], rows(Y1, to, 32, (1,)))
    sends["f2", 1] = (rows(feed, 16, 16, (1, 0)), rows(Y3, 8, 16, (1,)))
    sends["f2", -1] = (rows(feed, 0, 16, (1, 0)), rows(Y3, 56, 16, (1,)))
    copies = {name: send(name, *ends) for name, ends in sends.items()}

    def start(kind):
        for name in copies:
            if name[0] == kind:
                copies[name].start()

    def received(*kind):
        for name in copies:
            if name[: len(kind)] == kind:
                copies[name].wait_recv()

    fed1 = pltpu.make_async_copy(feed.at[0, 0], rows(Y1, 40, 32, (1,)), lsem.at[0])
    fed2 = pltpu.make_async_copy(feed.at[1, 0], rows(Y3, 24, 32, (1,)), lsem.at[1])
    fed3 = pltpu.make_async_copy(feed.at[2, 0], rows(Y5, 8, 32), lsem.at[2])

    pl.semaphore_wait(barrier, len(PEERS))
    start("v0")
    start("a")
    start("v1")
    start("v2")

    @pl.when(d == depths - 1)
    def _():
        start("f1")
        fed1.start()

    @pl.when(d == depths - 2)
    def _():
        start("f2")
        fed2.start()

    A[:, 48:80, :] = arr[0, 0]
    V0[:, 48:80, :] = vel[...]
    for copy in tabs:
        copy.wait()
    for k in range(4):
        for n in range(ORDER + 1):
            for part in (0, 1):
                line = TB[k, n, part]
                line = jnp.concatenate([line, line, line, line], axis=1)
                TW[k, 2 * n + part] = jnp.broadcast_to(line, (8, NY))

    total = strips * W
    middle = s * W + W // 2

    def step(count, src, lead, off, lev, row, base, tick, dst, dst_lead):
        tab = [TW[tick, i] for i in range(2 * ORDER + 2)]

        def load(c, j, nb):
            return src[(*lead, c, pl.ds(off + j, 8, stride=nb), slice(None))]

        def levels(j, nb):
            return lev[row, pl.ds(base + j, 8, stride=nb), :]

        def out(c, j, nb, value):
            dst[(*dst_lead, c, pl.ds(j, 8, stride=nb), slice(None))] = value

        layer(count, load, levels, tab, middle - count // 2, total, out)

    received("v0")
    received("a")
    step(ROWS[0], A, (), 0, V0, 0, 0, 0, Y0, ())
    step(ROWS[1], Y0, (), 8, V0, 1, 8, 0, Y1, (0,))
    received("v1")

    @pl.when(d == depths - 1)
    def _():
        received("f1")
        fed1.wait()

    last1 = jnp.where(d == depths - 1, 1, 0)
    step(ROWS[2], Y1, (last1,), 8, V1, 0, 0, 1, Y2, ())
    copies["i1", 0, 0].start()
    step(ROWS[3], Y2, (), 8, V1, 1, 8, 1, Y3, (0,))
    copies["i1", 1, 0].start()
    received("v2")

    @pl.when(d == depths - 2)
    def _():
        received("f2")
        fed2.wait()

    last2 = jnp.where(d == depths - 2, 1, 0)
    step(ROWS[4], Y3, (last2,), 8, V2, 0, 0, 2, Y4, ())
    copies["i2", 0, 0].start()
    step(ROWS[5], Y4, (), 8, V2, 1, 8, 2, Y5, ())

    @pl.when(d != depths - 3)
    def _():
        start("m")

    for name in ((0, 1, 0), (0, 1, 1), (0, 1, -1)):
        copies[("i2",) + name[1:]].start()

    @pl.when(d == depths - 3)
    def _():
        for name in ((1, 0), (1, 1), (1, -1)):
            copies[("i2",) + name].wait_send()
        fed3.start()
        fed3.wait()
        start("m")

    def image(sources, fresh):
        def body(k, carry):
            h = offs[k]
            for row in (0, 1):
                value = None if fresh else img[row, k]
                for ref, lead, at in sources[row]:
                    low = [ref[(*lead, c, pl.ds(at - h, W), slice(None))] for c in (0, 1)]
                    high = [ref[(*lead, c, pl.ds(at + h, W), slice(None))] for c in (2, 3)]
                    piece = low[0] * high[0] + low[1] * high[1]
                    value = piece if value is None else value + piece
                img[row, k] = value
            return carry

        lax.fori_loop(0, img.shape[1], body, 0)

    image([[(Y0, (), 48)], [(Y1, (0,), 40)]], True)
    received("i1")
    image([[(I1, (0,), 8)], [(I1, (1,), 8)]], False)
    received("i2")

    @pl.when(s == 0)
    def _():
        I2[1, :, 0:8, :] = jnp.zeros((4, 8, NY), F32)

    @pl.when(s == strips - 1)
    def _():
        I2[1, :, 40:48, :] = jnp.zeros((4, 8, NY), F32)

    image([[(I2, (0,), 8)], [(I2, (1,), 8)]], False)

    received("m")
    step(LAST[0], M, (), 0, V0, 0, 24, 3, Y6, ())
    step(LAST[1], Y6, (), 8, V0, 1, 32, 3, Y7, ())
    outflow[0, 0] = Y7[:, 16:48, :]
    image([[(Y6, (), 24)], [(Y7, (), 16)]], False)

    for name in copies:
        if name[0] in ("a", "v0", "v1", "v2", "i1", "m") or name == ("i2", 0, 0):
            copies[name].wait_send()

    @pl.when(d == depths - 1)
    def _():
        for shift in (1, -1):
            copies["f1", shift].wait_send()

    @pl.when(d == depths - 2)
    def _():
        for shift in (1, -1):
            copies["f2", shift].wait_send()

    @pl.when(d != depths - 3)
    def _():
        for name in ((1, 0), (1, 1), (1, -1)):
            copies[("i2",) + name].wait_send()


def solution(mesh):
    depths, strips = mesh.shape["depth"], mesh.shape["strip"]

    def per_device(arrivals, feed, velocity_index, offsets, coef_table):
        vmem = pl.BlockSpec(memory_space=pltpu.VMEM)
        field = lambda n, *lead: pltpu.VMEM((*lead, 4, n, NY), F32)
        level = lambda n: pltpu.VMEM((2, n, NY), jnp.int32)
        noff = offsets.shape[0]
        return pl.pallas_call(
            functools.partial(kernel, depths, strips),
            out_shape=(
                jax.ShapeDtypeStruct((2, noff, W, NY), F32),
                jax.ShapeDtypeStruct((1, 1, 4, W, NY), F32),
            ),
            in_specs=[vmem, vmem, pl.BlockSpec(memory_space=pltpu.SMEM), pl.BlockSpec(memory_space=pl.ANY), pl.BlockSpec(memory_space=pl.ANY)],
            out_specs=(vmem, vmem),
            scratch_shapes=[
                field(128), level(128), level(96), level(64),
                field(128), field(112, 2), field(96), field(80, 2), field(64), field(48), field(80), field(64),
                field(80), field(48, 2), field(48, 2),
                pltpu.VMEM((4, ORDER + 1, 2, 1, 32), F32),
                pltpu.VMEM((4, 2 * ORDER + 2, 8, NY), F32),
                pltpu.SemaphoreType.DMA((len(MSGS),)),
                pltpu.SemaphoreType.DMA((len(MSGS),)),
                pltpu.SemaphoreType.DMA((3,)),
                pltpu.SemaphoreType.DMA((4,)),
            ],
            compiler_params=pltpu.CompilerParams(collective_id=0, has_side_effects=True, vmem_limit_bytes=48 * 2**20),
            name="relay",
        )(arrivals, velocity_index, offsets, feed, coef_table)

    return jax.shard_map(
        per_device,
        mesh=mesh,
        in_specs=(
            P("depth", None, None, "strip", None),
            P(None, None, None, "strip", None),
            P("depth", "strip", None),
            P(),
            P(),
        ),
        out_specs=(P("depth", None, "strip", None), P("depth", None, None, "strip", None)),
        check_vma=False,
    )
```

time: 196 us -> 46.9 us (0.24)
  the two profiles are of different devices: /device:TPU:223 before, /device:TPU:1 now
where the time goes in v1:
time: 46.9 us; the launch traced here: 46.7 us
  Pallas kernels  43.4 us (93%)
  local copies, waits for them, and re-layouts  2.66 us (6%)
  between operations  0.7 us (1%)
    pallas_call x1, Pallas kernels, per_device(): pl.pallas_call(functools.partial(kernel, depths, strips), out_shape=(jax....  43.4 us
    unnamed x11, local copies, waits for them, and re-layouts  2.66 us

profile of v1, /device:TPU:1, one launch (start us, length us, event | category | flops | bytes accessed | tf_op | source)
XLA Modules:
  0.0 46.7 jit_solution(2888832226494230172)
XLA Ops:
  0.6 0.0 copy-start.3
  0.6 0.0 copy-start.2
  0.7 0.0 copy-start
  0.7 0.0 copy-start.1
  0.7 1.2 %copy.7.table = f32[35,9,2,1,32]{4,3,2,1,0:T(1,128)S(1)} copy(f32[35,9,2,1,32]{0,4,3,2,1:T(8,128)} %param.9) | data formatting | bytes 161280 | tf_op args[4]
  1.9 0.0 copy-done.3
  1.9 0.0 copy-done.2
  1.9 0.0 copy-done
  1.9 0.0 copy-done.1
  1.9 43.4 %relay.1 = (f32[2,16,32,128]{3,2,1,0:T(8,128)S(1)}, f32[1,1,4,32,128]{4,3,2,1,0:T(8,128)S(1)}) custom-call(f32[1,1,4,32,128]{4,3,2,1,0:T(8,128)S(1)} %copy-done.1, s32[2,32,128]{2,1,0:T(8,128)S(1)} %copy-done.2, s32[16]{0:T(128)S(1)} %copy-done.3, f32[3,1,4,32,128]{4,3,2,1,0:T(8,128)S(1)} %copy-done, f32[35,9,2,1,32]{4,3,2,1,0:T(1,128)S(1)} %copy.7.table), custom_call_target="tpu_custom_call" | custom-call | tf_op jit(solution)/shard_map/relay/pallas_call | solution.py:320
  45.3 0.8 %copy.10 = f32[2,16,32,128]{3,2,1,0:T(8,128)} copy(f32[2,16,32,128]{3,2,1,0:T(8,128)S(1)} %get-tuple-element.4) | data formatting | bytes 1048576
  46.1 0.6 %copy.11 = f32[1,1,4,32,128]{4,3,2,1,0:T(8,128)} copy(f32[1,1,4,32,128]{4,3,2,1,0:T(8,128)S(1)} %get-tuple-element.5) | data formatting | bytes 131072
Async XLA Ops:
  0.6 1.3 %copy-start.3 = (s32[16]{0:T(128)S(1)}, s32[16]{0:T(128)}, u32[]{:S(2)}) copy-start(s32[16]{0:T(128)} %offs.1) | copy-start | bytes 196
  0.6 1.3 %copy-start.2 = (s32[2,32,128]{2,1,0:T(8,128)S(1)}, s32[2,32,128]{2,1,0:T(8,128)}, u32[]{:S(2)}) copy-start(s32[2,32,128]{2,1,0:T(8,128)} %vel.1) | copy-start | bytes 98308
  0.7 1.3 %copy-start = (f32[3,1,4,32,128]{4,3,2,1,0:T(8,128)S(1)}, f32[3,1,4,32,128]{4,3,2,1,0:T(8,128)}, u32[]{:S(2)}) copy-start(f32[3,1,4,32,128]{4,3,2,1,0:T(8,128)} %feed.1) | copy-start | bytes 589828
  0.7 1.3 %copy-start.1 = (f32[1,1,4,32,128]{4,3,2,1,0:T(8,128)S(1)}, f32[1,1,4,32,128]{4,3,2,1,0:T(8,128)}, u32[]{:S(2)}) copy-start(f32[1,1,4,32,128]{4,3,2,1,0:T(8,128)} %arr.1) | copy-start | bytes 196612

commit v2 on v1

--- a/solution.py
+++ b/solution.py
@@ -11,6 +11,8 @@
 ORDER = 8
 W = 32
 NY = 128
+LEVELS = 32
+TABS = (2 * (ORDER + 1) * LEVELS + NY - 1) // NY
 F32 = jnp.float32
 
 ROWS = (128, 112, 96, 80, 64, 48)
@@ -74,10 +76,12 @@
         hist.append(t)
     for j in range(nb):
         idx = lev(j, nb)
+        idx = [idx + LEVELS * m for m in range(4)]
         acc = [None] * 4
         for n in range(ORDER + 1):
-            cr = jnp.take_along_axis(tab[2 * n], idx, axis=1)
-            ci = jnp.take_along_axis(tab[2 * n + 1], idx, axis=1)
+            cr, ci = [
+                jnp.take_along_axis(tab[c // 4], idx[c % 4], axis=1) for c in (2 * n, 2 * n + 1)
+            ]
             sr, si, rr, ri = [hist[n][c][j] for c in comps]
             new = [
                 cr * sr - ci * si,
@@ -90,25 +94,56 @@
             out(c, j, nb, acc[c])
 
 
-def kernel(depths, strips, arr, vel, offs, feed, table, img, outflow, A, V0, V1, V2, Y0, Y1, Y2, Y3, Y4, Y5, Y6, Y7, M, I1, I2, TB, TW, ssem, rsem, lsem, tsem):
+def kernel(depths, strips, arr, vel, offs, feed, table, img, outflow, A, V0, V1, V2, Y0, Y1, Y2, Y3, Y4, Y5, Y6, Y7, M, I1, I2, TC, TT, TW, ssem, rsem, lsem):
     d = lax.axis_index("depth")
     s = lax.axis_index("strip")
 
     def peer(shift):
         return (
             lax.rem(d + shift[0] + depths, depths),
-            lax.rem(s + shift[1] + strips, strips),
+            s + shift[1],
         )
 
+    def there(shift, sign=1):
+        if shift[1] == 0:
+            return None
+        at = s + sign * shift[1]
+        return (at >= 0) & (at < strips)
+
+    def guarded(condition, action):
+        if condition is None:
+            action()
+        else:
+            pl.when(condition)(action)
+
+    loads = [
+        pltpu.make_async_copy(table, TC, lsem.at[3]),
+        pltpu.make_async_copy(arr.at[0, 0], A.at[:, pl.ds(48, 32), :], lsem.at[4]),
+        pltpu.make_async_copy(vel, V0.at[:, pl.ds(48, 32), :], lsem.at[5]),
+    ]
+    for copy in loads:
+        copy.start()
+
+    @pl.when(s < 2)
+    def _():
+        V0[:, 0:48, :] = jnp.zeros((2, 48, NY), jnp.int32)
+        V1[:, 0:32, :] = jnp.zeros((2, 32, NY), jnp.int32)
+        V2[:, 0:16, :] = jnp.zeros((2, 16, NY), jnp.int32)
+
+    @pl.when(s >= strips - 2)
+    def _():
+        V0[:, 80:128, :] = jnp.zeros((2, 48, NY), jnp.int32)
+        V1[:, 64:96, :] = jnp.zeros((2, 32, NY), jnp.int32)
+        V2[:, 48:64, :] = jnp.zeros((2, 16, NY), jnp.int32)
+
     barrier = pltpu.get_barrier_semaphore()
+    expected = 0
     for shift in PEERS:
-        pl.semaphore_signal(barrier, inc=1, device_id=peer((-shift[0], -shift[1])), device_id_type=MESH)
-
-    wraps = [d + k >= depths for k in range(3)]
-    tick_row = [jnp.where(wraps[k], 2 * depths - 1 - d, depths - 1 - d) for k in range(3)] + [depths + 2 - d]
-    tabs = [pltpu.make_async_copy(table.at[tick_row[k]], TB.at[k], tsem.at[k]) for k in range(4)]
-    for copy in tabs:
-        copy.start()
+        def greet(shift=shift):
+            pl.semaphore_signal(barrier, inc=1, device_id=peer((-shift[0], -shift[1])), device_id_type=MESH)
+
+        guarded(there(shift, -1), greet)
+        expected = expected + (1 if shift[1] == 0 else jnp.where(there(shift), 1, 0))
 
     def send(name, src, dst):
         i = INDEX[name]
@@ -155,18 +190,21 @@
     def start(kind):
         for name in copies:
             if name[0] == kind:
-                copies[name].start()
+                guarded(there(MSGS[name]), copies[name].start)
 
     def received(*kind):
         for name in copies:
             if name[: len(kind)] == kind:
-                copies[name].wait_recv()
+                guarded(there(MSGS[name], -1), copies[name].wait_recv)
+
+    def sent(name):
+        guarded(there(MSGS[name]), copies[name].wait_send)
 
     fed1 = pltpu.make_async_copy(feed.at[0, 0], rows(Y1, 40, 32, (1,)), lsem.at[0])
     fed2 = pltpu.make_async_copy(feed.at[1, 0], rows(Y3, 24, 32, (1,)), lsem.at[1])
     fed3 = pltpu.make_async_copy(feed.at[2, 0], rows(Y5, 8, 32), lsem.at[2])
 
-    pl.semaphore_wait(barrier, len(PEERS))
+    pl.semaphore_wait(barrier, expected)
     start("v0")
     start("a")
     start("v1")
@@ -182,22 +220,24 @@
         start("f2")
         fed2.start()
 
-    A[:, 48:80, :] = arr[0, 0]
-    V0[:, 48:80, :] = vel[...]
-    for copy in tabs:
+    for copy in loads:
         copy.wait()
+    turned = TC[...].T
+    for g in range(TABS):
+        width = min(NY, table.shape[0] - g * NY)
+        TT[g, :, 0:width] = turned[:, g * NY : g * NY + width]
+    wraps = [d + k >= depths for k in range(3)]
+    tick_row = [jnp.where(wraps[k], 2 * depths - 1 - d, depths - 1 - d) for k in range(3)] + [depths + 2 - d]
     for k in range(4):
-        for n in range(ORDER + 1):
-            for part in (0, 1):
-                line = TB[k, n, part]
-                line = jnp.concatenate([line, line, line, line], axis=1)
-                TW[k, 2 * n + part] = jnp.broadcast_to(line, (8, NY))
+        for g in range(TABS):
+            line = TT[g, pl.ds(tick_row[k], 1), :]
+            TW[k, g] = jnp.broadcast_to(line, (8, NY))
 
     total = strips * W
     middle = s * W + W // 2
 
     def step(count, src, lead, off, lev, row, base, tick, dst, dst_lead):
-        tab = [TW[tick, i] for i in range(2 * ORDER + 2)]
+        tab = [TW[tick, g] for g in range(TABS)]
 
         def load(c, j, nb):
             return src[(*lead, c, pl.ds(off + j, 8, stride=nb), slice(None))]
@@ -243,12 +283,12 @@
         start("m")
 
     for name in ((0, 1, 0), (0, 1, 1), (0, 1, -1)):
-        copies[("i2",) + name[1:]].start()
+        guarded(there(MSGS[("i2",) + name[1:]]), copies[("i2",) + name[1:]].start)
 
     @pl.when(d == depths - 3)
     def _():
         for name in ((1, 0), (1, 1), (1, -1)):
-            copies[("i2",) + name].wait_send()
+            sent(("i2",) + name)
         fed3.start()
         fed3.wait()
         start("m")
@@ -291,22 +331,22 @@
 
     for name in copies:
         if name[0] in ("a", "v0", "v1", "v2", "i1", "m") or name == ("i2", 0, 0):
-            copies[name].wait_send()
+            sent(name)
 
     @pl.when(d == depths - 1)
     def _():
         for shift in (1, -1):
-            copies["f1", shift].wait_send()
+            sent(("f1", shift))
 
     @pl.when(d == depths - 2)
     def _():
         for shift in (1, -1):
-            copies["f2", shift].wait_send()
+            sent(("f2", shift))
 
     @pl.when(d != depths - 3)
     def _():
         for name in ((1, 0), (1, 1), (1, -1)):
-            copies[("i2",) + name].wait_send()
+            sent(("i2",) + name)
 
 
 def solution(mesh):
@@ -314,31 +354,33 @@
 
     def per_device(arrivals, feed, velocity_index, offsets, coef_table):
         vmem = pl.BlockSpec(memory_space=pltpu.VMEM)
+        anyw = pl.BlockSpec(memory_space=pl.ANY)
         field = lambda n, *lead: pltpu.VMEM((*lead, 4, n, NY), F32)
         level = lambda n: pltpu.VMEM((2, n, NY), jnp.int32)
         noff = offsets.shape[0]
+        columns = jnp.transpose(coef_table, (1, 2, 3, 4, 0)).reshape(-1, coef_table.shape[0])
         return pl.pallas_call(
             functools.partial(kernel, depths, strips),
             out_shape=(
                 jax.ShapeDtypeStruct((2, noff, W, NY), F32),
                 jax.ShapeDtypeStruct((1, 1, 4, W, NY), F32),
             ),
-            in_specs=[vmem, vmem, pl.BlockSpec(memory_space=pltpu.SMEM), pl.BlockSpec(memory_space=pl.ANY), pl.BlockSpec(memory_space=pl.ANY)],
+            in_specs=[anyw, anyw, pl.BlockSpec(memory_space=pltpu.SMEM), anyw, anyw],
             out_specs=(vmem, vmem),
             scratch_shapes=[
                 field(128), level(128), level(96), level(64),
                 field(128), field(112, 2), field(96), field(80, 2), field(64), field(48), field(80), field(64),
                 field(80), field(48, 2), field(48, 2),
-                pltpu.VMEM((4, ORDER + 1, 2, 1, 32), F32),
-                pltpu.VMEM((4, 2 * ORDER + 2, 8, NY), F32),
+                pltpu.VMEM(columns.shape, F32),
+                pltpu.VMEM((TABS, coef_table.shape[0], NY), F32),
+                pltpu.VMEM((4, TABS, 8, NY), F32),
                 pltpu.SemaphoreType.DMA((len(MSGS),)),
                 pltpu.SemaphoreType.DMA((len(MSGS),)),
-                pltpu.SemaphoreType.DMA((3,)),
-                pltpu.SemaphoreType.DMA((4,)),
+                pltpu.SemaphoreType.DMA((6,)),
             ],
-            compiler_params=pltpu.CompilerParams(collective_id=0, has_side_effects=True, vmem_limit_bytes=48 * 2**20),
+            compiler_params=pltpu.CompilerParams(collective_id=0, has_side_effects=True, vmem_limit_bytes=60 * 2**20),
             name="relay",
-        )(arrivals, velocity_index, offsets, feed, coef_table)
+        )(arrivals, velocity_index, offsets, feed, columns)
 
     return jax.shard_map(
         per_device,

time: 46.9 us -> 46.3 us (0.987)
  Pallas kernels: 43.4 us -> 42.9 us
    unnamed x11 -> x4, local copies, waits for them, and re-layouts: 2.66 us -> 2.53 us
where the time goes in v2:
time: 46.3 us; the launch traced here: 46.1 us
  Pallas kernels  42.9 us (93%)
  local copies, waits for them, and re-layouts  2.53 us (5%)
  between operations  0.65 us (1%)
    pallas_call x1, Pallas kernels, per_device(): pl.pallas_call(functools.partial(kernel, depths, strips), out_shape=(jax....  42.9 us
    unnamed x4, local copies, waits for them, and re-layouts  2.53 us

profile of v2, /device:TPU:1, one launch (start us, length us, event | category | flops | bytes accessed | tf_op | source)
XLA Modules:
  0.0 46.1 jit_solution(11274285734803420261)
XLA Ops:
  0.6 42.9 %relay.1 = (f32[2,16,32,128]{3,2,1,0:T(8,128)}, f32[1,1,4,32,128]{4,3,2,1,0:T(8,128)}) custom-call(f32[1,1,4,32,128]{4,3,2,1,0:T(8,128)} %arr.1, s32[2,32,128]{2,1,0:T(8,128)} %vel.1, s32[16]{0:T(128)} %offs.1, f32[3,1,4,32,128]{4,3,2,1,0:T(8,128)} %feed.1, f32[576,35]{1,0:T(8,128)} %bitcast.3), custom_call_target="tpu_custom_call" | custom-call | tf_op jit(solution)/shard_map/relay/pallas_call | solution.py:362
  43.6 0.0 copy-start
  43.6 1.9 %copy.9 = f32[2,16,32,128]{3,2,1,0:T(8,128)} copy(f32[2,16,32,128]{3,2,1,0:T(8,128)} %get-tuple-element.4) | data formatting | bytes 1048576
  45.5 0.0 copy-done
  45.5 0.6 %copy.10 = f32[1,1,4,32,128]{4,3,2,1,0:T(8,128)} copy(f32[1,1,4,32,128]{4,3,2,1,0:T(8,128)S(1)} %copy-done) | data formatting | bytes 131072
Async XLA Ops:
  43.6 1.9 %copy-start = (f32[1,1,4,32,128]{4,3,2,1,0:T(8,128)S(1)}, f32[1,1,4,32,128]{4,3,2,1,0:T(8,128)}, u32[]{:S(2)}) copy-start(f32[1,1,4,32,128]{4,3,2,1,0:T(8,128)} %get-tuple-element.5) | copy-start | bytes 196612

commit v3 on v2

--- a/solution.py
+++ b/solution.py
@@ -37,7 +37,13 @@
 PEERS = sorted(set(MSGS.values()))
 
 
-def layer(rows, load, lev, tab, top, total, out):
+def looked_up(nb, lev, tab, j):
+    idx = lev(j, nb)
+    idx = [idx + LEVELS * m for m in range(4)]
+    return [jnp.take_along_axis(tab[c // 4], idx[c % 4], axis=1) for c in range(2 * ORDER + 2)]
+
+
+def layer(rows, load, coefs, top, total, out):
     nb = rows // 8
     lanes = lax.broadcasted_iota(jnp.int32, (8, NY), 1)
     first, final = lanes == 0, lanes == NY - 1
@@ -75,13 +81,10 @@
         t, p = new_t, new_p
         hist.append(t)
     for j in range(nb):
-        idx = lev(j, nb)
-        idx = [idx + LEVELS * m for m in range(4)]
+        chosen = coefs(j)
         acc = [None] * 4
         for n in range(ORDER + 1):
-            cr, ci = [
-                jnp.take_along_axis(tab[c // 4], idx[c % 4], axis=1) for c in (2 * n, 2 * n + 1)
-            ]
+            cr, ci = chosen[2 * n], chosen[2 * n + 1]
             sr, si, rr, ri = [hist[n][c][j] for c in comps]
             new = [
                 cr * sr - ci * si,
@@ -94,7 +97,40 @@
             out(c, j, nb, acc[c])
 
 
-def kernel(depths, strips, arr, vel, offs, feed, table, img, outflow, A, V0, V1, V2, Y0, Y1, Y2, Y3, Y4, Y5, Y6, Y7, M, I1, I2, TC, TT, TW, ssem, rsem, lsem):
+def product(ref, lead, at, h):
+    low = [ref[(*lead, c, pl.ds(at - h, W), slice(None))] for c in (0, 1)]
+    high = [ref[(*lead, c, pl.ds(at + h, W), slice(None))] for c in (2, 3)]
+    return low[0] * high[0] + low[1] * high[1]
+
+
+def finish(partial, last, offs, image, outflow, out, fields, sem):
+    loads = [
+        pltpu.make_async_copy(last.at[0], fields.at[0], sem.at[0]),
+        pltpu.make_async_copy(last.at[1], fields.at[1], sem.at[1]),
+        pltpu.make_async_copy(partial.at[0], out.at[0], sem.at[2]),
+        pltpu.make_async_copy(partial.at[1], out.at[1], sem.at[3]),
+    ]
+    for copy in loads:
+        copy.start()
+    loads[1].wait()
+    stores = [pltpu.make_async_copy(fields.at[1, :, pl.ds(8, W), :], outflow.at[0, 0], sem.at[6])]
+    stores[0].start()
+    loads[0].wait()
+    for row in (0, 1):
+        loads[2 + row].wait()
+
+        def body(k, carry):
+            out[row, k] = out[row, k] + product(fields, (row,), 8, offs[k])
+            return carry
+
+        lax.fori_loop(0, out.shape[1], body, 0)
+        stores.append(pltpu.make_async_copy(out.at[row], image.at[row], sem.at[4 + row]))
+        stores[-1].start()
+    for copy in stores:
+        copy.wait()
+
+
+def kernel(depths, strips, arr, vel, offs, feed, table, img_out, last_out, img, A, V0, V1, V2, Y0, Y1, Y2, Y3, Y4, Y5, Y6, Y7, M, I1, I2, TC, TT, TW, C6, C7, ssem, rsem, lsem):
     d = lax.axis_index("depth")
     s = lax.axis_index("strip")
 
@@ -236,24 +272,28 @@
     total = strips * W
     middle = s * W + W // 2
 
-    def step(count, src, lead, off, lev, row, base, tick, dst, dst_lead):
+    def lookup(count, lev, row, base, tick):
         tab = [TW[tick, g] for g in range(TABS)]
+
+        def levels(j, nb):
+            return lev[row, pl.ds(base + j, 8, stride=nb), :]
+
+        return lambda j: looked_up(count // 8, levels, tab, j)
+
+    def step(count, src, lead, off, coefs, dst, dst_lead):
 
         def load(c, j, nb):
             return src[(*lead, c, pl.ds(off + j, 8, stride=nb), slice(None))]
 
-        def levels(j, nb):
-            return lev[row, pl.ds(base + j, 8, stride=nb), :]
-
         def out(c, j, nb, value):
             dst[(*dst_lead, c, pl.ds(j, 8, stride=nb), slice(None))] = value
 
-        layer(count, load, levels, tab, middle - count // 2, total, out)
+        layer(count, load, coefs, middle - count // 2, total, out)
 
     received("v0")
     received("a")
-    step(ROWS[0], A, (), 0, V0, 0, 0, 0, Y0, ())
-    step(ROWS[1], Y0, (), 8, V0, 1, 8, 0, Y1, (0,))
+    step(ROWS[0], A, (), 0, lookup(ROWS[0], V0, 0, 0, 0), Y0, ())
+    step(ROWS[1], Y0, (), 8, lookup(ROWS[1], V0, 1, 8, 0), Y1, (0,))
     received("v1")
 
     @pl.when(d == depths - 1)
@@ -262,9 +302,9 @@
         fed1.wait()
 
     last1 = jnp.where(d == depths - 1, 1, 0)
-    step(ROWS[2], Y1, (last1,), 8, V1, 0, 0, 1, Y2, ())
+    step(ROWS[2], Y1, (last1,), 8, lookup(ROWS[2], V1, 0, 0, 1), Y2, ())
     copies["i1", 0, 0].start()
-    step(ROWS[3], Y2, (), 8, V1, 1, 8, 1, Y3, (0,))
+    step(ROWS[3], Y2, (), 8, lookup(ROWS[3], V1, 1, 8, 1), Y3, (0,))
     copies["i1", 1, 0].start()
     received("v2")
 
@@ -274,14 +314,14 @@
         fed2.wait()
 
     last2 = jnp.where(d == depths - 2, 1, 0)
-    step(ROWS[4], Y3, (last2,), 8, V2, 0, 0, 2, Y4, ())
+    step(ROWS[4], Y3, (last2,), 8, lookup(ROWS[4], V2, 0, 0, 2), Y4, ())
+    step(ROWS[5], Y4, (), 8, lookup(ROWS[5], V2, 1, 8, 2), Y5, ())
+
+    @pl.when(d != depths - 3)
+    def _():
+        start("m")
+
     copies["i2", 0, 0].start()
-    step(ROWS[5], Y4, (), 8, V2, 1, 8, 2, Y5, ())
-
-    @pl.when(d != depths - 3)
-    def _():
-        start("m")
-
     for name in ((0, 1, 0), (0, 1, 1), (0, 1, -1)):
         guarded(there(MSGS[("i2",) + name[1:]]), copies[("i2",) + name[1:]].start)
 
@@ -295,22 +335,39 @@
 
     def image(sources, fresh):
         def body(k, carry):
-            h = offs[k]
             for row in (0, 1):
                 value = None if fresh else img[row, k]
-                for ref, lead, at in sources[row]:
-                    low = [ref[(*lead, c, pl.ds(at - h, W), slice(None))] for c in (0, 1)]
-                    high = [ref[(*lead, c, pl.ds(at + h, W), slice(None))] for c in (2, 3)]
-                    piece = low[0] * high[0] + low[1] * high[1]
+                for source in sources[row]:
+                    piece = product(*source, offs[k])
                     value = piece if value is None else value + piece
                 img[row, k] = value
             return carry
 
         lax.fori_loop(0, img.shape[1], body, 0)
 
+    def keep(ref, count, row, base):
+        get = lookup(count, V0, row, base, 3)
+        for j in range(count // 8):
+            for c, value in enumerate(get(j)):
+                ref[c, j] = value
+
+    def kept(ref, count):
+        return lambda j: [ref[c, j] for c in range(2 * ORDER + 2)]
+
+    keep(C6, LAST[0], 0, 24)
+    keep(C7, LAST[1], 1, 32)
     image([[(Y0, (), 48)], [(Y1, (0,), 40)]], True)
     received("i1")
     image([[(I1, (0,), 8)], [(I1, (1,), 8)]], False)
+    lasts_out = [
+        pltpu.make_async_copy(Y6.at[:, pl.ds(16, W + 16), :], last_out.at[0], lsem.at[7]),
+        pltpu.make_async_copy(Y7.at[:, pl.ds(8, W + 16), :], last_out.at[1], lsem.at[8]),
+    ]
+    received("m")
+    step(LAST[0], M, (), 0, kept(C6, LAST[0]), Y6, ())
+    lasts_out[0].start()
+    step(LAST[1], Y6, (), 8, kept(C7, LAST[1]), Y7, ())
+    lasts_out[1].start()
     received("i2")
 
     @pl.when(s == 0)
@@ -322,12 +379,12 @@
         I2[1, :, 40:48, :] = jnp.zeros((4, 8, NY), F32)
 
     image([[(I2, (0,), 8)], [(I2, (1,), 8)]], False)
-
-    received("m")
-    step(LAST[0], M, (), 0, V0, 0, 24, 3, Y6, ())
-    step(LAST[1], Y6, (), 8, V0, 1, 32, 3, Y7, ())
-    outflow[0, 0] = Y7[:, 16:48, :]
-    image([[(Y6, (), 24)], [(Y7, (), 16)]], False)
+    partial_out = pltpu.make_async_copy(img, img_out, lsem.at[6])
+    partial_out.start()
+
+    partial_out.wait()
+    for copy in lasts_out:
+        copy.wait()
 
     for name in copies:
         if name[0] in ("a", "v0", "v1", "v2", "i1", "m") or name == ("i2", 0, 0):
@@ -353,34 +410,53 @@
     depths, strips = mesh.shape["depth"], mesh.shape["strip"]
 
     def per_device(arrivals, feed, velocity_index, offsets, coef_table):
-        vmem = pl.BlockSpec(memory_space=pltpu.VMEM)
-        anyw = pl.BlockSpec(memory_space=pl.ANY)
+        hbm = pl.BlockSpec(memory_space=pltpu.HBM)
+        smem = pl.BlockSpec(memory_space=pltpu.SMEM)
         field = lambda n, *lead: pltpu.VMEM((*lead, 4, n, NY), F32)
         level = lambda n: pltpu.VMEM((2, n, NY), jnp.int32)
         noff = offsets.shape[0]
         columns = jnp.transpose(coef_table, (1, 2, 3, 4, 0)).reshape(-1, coef_table.shape[0])
-        return pl.pallas_call(
+        partial, last = pl.pallas_call(
             functools.partial(kernel, depths, strips),
             out_shape=(
                 jax.ShapeDtypeStruct((2, noff, W, NY), F32),
-                jax.ShapeDtypeStruct((1, 1, 4, W, NY), F32),
+                jax.ShapeDtypeStruct((2, 4, W + 16, NY), F32),
             ),
-            in_specs=[anyw, anyw, pl.BlockSpec(memory_space=pltpu.SMEM), anyw, anyw],
-            out_specs=(vmem, vmem),
+            in_specs=[hbm, hbm, smem, hbm, hbm],
+            out_specs=(hbm, hbm),
             scratch_shapes=[
+                pltpu.VMEM((2, noff, W, NY), F32),
                 field(128), level(128), level(96), level(64),
                 field(128), field(112, 2), field(96), field(80, 2), field(64), field(48), field(80), field(64),
                 field(80), field(48, 2), field(48, 2),
                 pltpu.VMEM(columns.shape, F32),
                 pltpu.VMEM((TABS, coef_table.shape[0], NY), F32),
                 pltpu.VMEM((4, TABS, 8, NY), F32),
+                pltpu.VMEM((2 * ORDER + 2, LAST[0] // 8, 8, NY), F32),
+                pltpu.VMEM((2 * ORDER + 2, LAST[1] // 8, 8, NY), F32),
                 pltpu.SemaphoreType.DMA((len(MSGS),)),
                 pltpu.SemaphoreType.DMA((len(MSGS),)),
-                pltpu.SemaphoreType.DMA((6,)),
+                pltpu.SemaphoreType.DMA((9,)),
             ],
             compiler_params=pltpu.CompilerParams(collective_id=0, has_side_effects=True, vmem_limit_bytes=60 * 2**20),
             name="relay",
         )(arrivals, velocity_index, offsets, feed, columns)
+        return pl.pallas_call(
+            finish,
+            out_shape=(
+                jax.ShapeDtypeStruct((2, noff, W, NY), F32),
+                jax.ShapeDtypeStruct((1, 1, 4, W, NY), F32),
+            ),
+            in_specs=[hbm, hbm, smem],
+            out_specs=(hbm, hbm),
+            scratch_shapes=[
+                pltpu.VMEM((2, noff, W, NY), F32),
+                pltpu.VMEM((2, 4, W + 16, NY), F32),
+                pltpu.SemaphoreType.DMA((7,)),
+            ],
+            compiler_params=pltpu.CompilerParams(vmem_limit_bytes=60 * 2**20),
+            name="finish",
+        )(partial, last, offsets)
 
     return jax.shard_map(
         per_device,

time: 46.3 us -> 46.9 us (1.013)
  Pallas kernels: 42.9 us -> 45.9 us
  local copies, waits for them, and re-layouts: 2.53 us -> 0 us
    pallas_call x0 -> x1, Pallas kernels: none -> 2.81 us  [per_device(): pl.pallas_call(finish, out_shape=(jax.ShapeDtypeStruct((2, noff, W, NY),...]
    unnamed x4 -> x0, local copies, waits for them, and re-layouts: 2.53 us -> none
where the time goes in v3:
time: 46.9 us; the launch traced here: 46.6 us
  Pallas kernels  45.9 us (98%)
  between operations  0.64 us (1%)
    pallas_call x1, Pallas kernels, per_device(): pl.pallas_call(functools.partial(kernel, depths, strips), out_shape=(jax....  43.1 us
    pallas_call x1, Pallas kernels, per_device(): pl.pallas_call(finish, out_shape=(jax.ShapeDtypeStruct((2, noff, W, NY),...  2.81 us

profile of v3, /device:TPU:1, one launch (start us, length us, event | category | flops | bytes accessed | tf_op | source)
XLA Modules:
  0.0 46.6 jit_solution(11195670475071741391)
XLA Ops:
  0.6 43.1 %relay.1 = (f32[2,16,32,128]{3,2,1,0:T(8,128)}, f32[2,4,48,128]{3,2,1,0:T(8,128)}) custom-call(f32[1,1,4,32,128]{4,3,2,1,0:T(8,128)} %arr.1, s32[2,32,128]{2,1,0:T(8,128)} %vel.1, s32[16]{0:T(128)} %offs.3, f32[3,1,4,32,128]{4,3,2,1,0:T(8,128)} %feed.1, f32[576,35]{1,0:T(8,128)} %bitcast.3), custom_call_target="tpu_custom_call" | custom-call | tf_op jit(solution)/shard_map/relay/pallas_call | solution.py:419
  43.8 2.8 %finish.1 = (f32[2,16,32,128]{3,2,1,0:T(8,128)}, f32[1,1,4,32,128]{4,3,2,1,0:T(8,128)}) custom-call(f32[2,16,32,128]{3,2,1,0:T(8,128)} %get-tuple-element.4.partial, f32[2,4,48,128]{3,2,1,0:T(8,128)} %get-tuple-element.5.last, s32[16]{0:T(128)} %offs.3), custom_call_target="tpu_custom_call" | custom-call | tf_op jit(solution)/shard_map/finish/pallas_call | solution.py:444

commit v4 on v3

--- a/solution.py
+++ b/solution.py
@@ -10,6 +10,7 @@
 MESH = pl.DeviceIdType.MESH
 ORDER = 8
 W = 32
+PARTS = 4
 NY = 128
 LEVELS = 32
 TABS = (2 * (ORDER + 1) * LEVELS + NY - 1) // NY
@@ -103,34 +104,38 @@
     return low[0] * high[0] + low[1] * high[1]
 
 
-def finish(partial, last, offs, image, outflow, out, fields, sem):
-    loads = [
-        pltpu.make_async_copy(last.at[0], fields.at[0], sem.at[0]),
-        pltpu.make_async_copy(last.at[1], fields.at[1], sem.at[1]),
-        pltpu.make_async_copy(partial.at[0], out.at[0], sem.at[2]),
-        pltpu.make_async_copy(partial.at[1], out.at[1], sem.at[3]),
-    ]
-    for copy in loads:
+def finish(partial, last, second, offs, image, outflow, out, fields, sem):
+    loads = {}
+    for row in (1, 0):
+        loads["last", row] = (last.at[row], fields.at[0, row])
+    for row in (0, 1):
+        loads["second", row] = (second.at[row], fields.at[1, row])
+        for part in range(PARTS):
+            some = pl.ds(part * out.shape[1] // PARTS, out.shape[1] // PARTS)
+            loads[row, part] = (partial.at[row, some], out.at[row, some])
+    loads = {name: pltpu.make_async_copy(*ends, sem.at[i]) for i, (name, ends) in enumerate(loads.items())}
+    for copy in loads.values():
         copy.start()
-    loads[1].wait()
-    stores = [pltpu.make_async_copy(fields.at[1, :, pl.ds(8, W), :], outflow.at[0, 0], sem.at[6])]
+    loads["last", 1].wait()
+    stores = [pltpu.make_async_copy(fields.at[0, 1, :, pl.ds(8, W), :], outflow.at[0, 0], sem.at[len(loads)])]
     stores[0].start()
-    loads[0].wait()
+    loads["last", 0].wait()
     for row in (0, 1):
-        loads[2 + row].wait()
-
-        def body(k, carry):
-            out[row, k] = out[row, k] + product(fields, (row,), 8, offs[k])
-            return carry
-
-        lax.fori_loop(0, out.shape[1], body, 0)
-        stores.append(pltpu.make_async_copy(out.at[row], image.at[row], sem.at[4 + row]))
-        stores[-1].start()
+        loads["second", row].wait()
+        for part in range(PARTS):
+            loads[row, part].wait()
+            first, count = part * out.shape[1] // PARTS, out.shape[1] // PARTS
+            for k in range(first, first + count):
+                h = offs[k]
+                out[row, k] = out[row, k] + product(fields, (0, row), 8, h) + product(fields, (1, row), 8, h)
+            some = pl.ds(first, count)
+            stores.append(pltpu.make_async_copy(out.at[row, some], image.at[row, some], sem.at[len(loads) + len(stores)]))
+            stores[-1].start()
     for copy in stores:
         copy.wait()
 
 
-def kernel(depths, strips, arr, vel, offs, feed, table, img_out, last_out, img, A, V0, V1, V2, Y0, Y1, Y2, Y3, Y4, Y5, Y6, Y7, M, I1, I2, TC, TT, TW, C6, C7, ssem, rsem, lsem):
+def kernel(depths, strips, arr, vel, offs, feed, table, img_out, last_out, second, img, A, V0, V1, V2, Y0, Y1, Y2, Y3, Y4, Y5, Y6, Y7, M, I1, I2, TC, TT, TW, C6, C7, ssem, rsem, lsem):
     d = lax.axis_index("depth")
     s = lax.axis_index("strip")
 
@@ -238,7 +243,9 @@
 
     fed1 = pltpu.make_async_copy(feed.at[0, 0], rows(Y1, 40, 32, (1,)), lsem.at[0])
     fed2 = pltpu.make_async_copy(feed.at[1, 0], rows(Y3, 24, 32, (1,)), lsem.at[1])
-    fed3 = pltpu.make_async_copy(feed.at[2, 0], rows(Y5, 8, 32), lsem.at[2])
+    entering = {}
+    for shift, (at, count, to) in moved.items():
+        entering[shift] = send(("m", shift), rows(feed, at - 8, count, (2, 0)), rows(M, to, count))
 
     pl.semaphore_wait(barrier, expected)
     start("v0")
@@ -255,6 +262,11 @@
     def _():
         start("f2")
         fed2.start()
+
+    @pl.when(d == depths - 3)
+    def _():
+        for shift, copy in entering.items():
+            guarded(there(MSGS["m", shift]), copy.start)
 
     for copy in loads:
         copy.wait()
@@ -321,17 +333,7 @@
     def _():
         start("m")
 
-    copies["i2", 0, 0].start()
-    for name in ((0, 1, 0), (0, 1, 1), (0, 1, -1)):
-        guarded(there(MSGS[("i2",) + name[1:]]), copies[("i2",) + name[1:]].start)
-
-    @pl.when(d == depths - 3)
-    def _():
-        for name in ((1, 0), (1, 1), (1, -1)):
-            sent(("i2",) + name)
-        fed3.start()
-        fed3.wait()
-        start("m")
+    start("i2")
 
     def image(sources, fresh):
         def body(k, carry):
@@ -359,6 +361,8 @@
     image([[(Y0, (), 48)], [(Y1, (0,), 40)]], True)
     received("i1")
     image([[(I1, (0,), 8)], [(I1, (1,), 8)]], False)
+    partial_out = pltpu.make_async_copy(img, img_out, lsem.at[6])
+    partial_out.start()
     lasts_out = [
         pltpu.make_async_copy(Y6.at[:, pl.ds(16, W + 16), :], last_out.at[0], lsem.at[7]),
         pltpu.make_async_copy(Y7.at[:, pl.ds(8, W + 16), :], last_out.at[1], lsem.at[8]),
@@ -378,16 +382,16 @@
     def _():
         I2[1, :, 40:48, :] = jnp.zeros((4, 8, NY), F32)
 
-    image([[(I2, (0,), 8)], [(I2, (1,), 8)]], False)
-    partial_out = pltpu.make_async_copy(img, img_out, lsem.at[6])
-    partial_out.start()
+    second_out = pltpu.make_async_copy(I2, second, lsem.at[2])
+    second_out.start()
 
     partial_out.wait()
+    second_out.wait()
     for copy in lasts_out:
         copy.wait()
 
     for name in copies:
-        if name[0] in ("a", "v0", "v1", "v2", "i1", "m") or name == ("i2", 0, 0):
+        if name[0] in ("a", "v0", "v1", "v2", "i1", "i2", "m"):
             sent(name)
 
     @pl.when(d == depths - 1)
@@ -399,11 +403,6 @@
     def _():
         for shift in (1, -1):
             sent(("f2", shift))
-
-    @pl.when(d != depths - 3)
-    def _():
-        for name in ((1, 0), (1, 1), (1, -1)):
-            sent(("i2",) + name)
 
 
 def solution(mesh):
@@ -416,14 +415,15 @@
         level = lambda n: pltpu.VMEM((2, n, NY), jnp.int32)
         noff = offsets.shape[0]
         columns = jnp.transpose(coef_table, (1, 2, 3, 4, 0)).reshape(-1, coef_table.shape[0])
-        partial, last = pl.pallas_call(
+        partial, last, second = pl.pallas_call(
             functools.partial(kernel, depths, strips),
             out_shape=(
                 jax.ShapeDtypeStruct((2, noff, W, NY), F32),
                 jax.ShapeDtypeStruct((2, 4, W + 16, NY), F32),
+                jax.ShapeDtypeStruct((2, 4, W + 16, NY), F32),
             ),
             in_specs=[hbm, hbm, smem, hbm, hbm],
-            out_specs=(hbm, hbm),
+            out_specs=(hbm, hbm, hbm),
             scratch_shapes=[
                 pltpu.VMEM((2, noff, W, NY), F32),
                 field(128), level(128), level(96), level(64),
@@ -447,16 +447,16 @@
                 jax.ShapeDtypeStruct((2, noff, W, NY), F32),
                 jax.ShapeDtypeStruct((1, 1, 4, W, NY), F32),
             ),
-            in_specs=[hbm, hbm, smem],
+            in_specs=[hbm, hbm, hbm, smem],
             out_specs=(hbm, hbm),
             scratch_shapes=[
                 pltpu.VMEM((2, noff, W, NY), F32),
-                pltpu.VMEM((2, 4, W + 16, NY), F32),
-                pltpu.SemaphoreType.DMA((7,)),
+                pltpu.VMEM((2, 2, 4, W + 16, NY), F32),
+                pltpu.SemaphoreType.DMA((4 * PARTS + 5,)),
             ],
             compiler_params=pltpu.CompilerParams(vmem_limit_bytes=60 * 2**20),
             name="finish",
-        )(partial, last, offsets)
+        )(partial, last, second, offsets)
 
     return jax.shard_map(
         per_device,

time: 46.9 us -> 41.3 us (0.88)
  the two profiles are of different devices: /device:TPU:1 before, /device:TPU:67 now
where the time goes in v4:
time: 41.3 us; the launch traced here: 41.1 us
  Pallas kernels  40.5 us (98%)
  between operations  0.64 us (2%)
    pallas_call x1, Pallas kernels, per_device(): pl.pallas_call(functools.partial(kernel, depths, strips), out_shape=(jax....  37.6 us
    pallas_call x1, Pallas kernels, per_device(): pl.pallas_call(finish, out_shape=(jax.ShapeDtypeStruct((2, noff, W, NY),...  2.89 us

profile of v4, /device:TPU:67, one launch (start us, length us, event | category | flops | bytes accessed | tf_op | source)
XLA Modules:
  0.0 41.1 jit_solution(11712050171414593736)
XLA Ops:
  0.6 37.6 %relay.1 = (f32[2,16,32,128]{3,2,1,0:T(8,128)}, f32[2,4,48,128]{3,2,1,0:T(8,128)}, f32[2,4,48,128]{3,2,1,0:T(8,128)}) custom-call(f32[1,1,4,32,128]{4,3,2,1,0:T(8,128)} %arr.1, s32[2,32,128]{2,1,0:T(8,128)} %vel.1, s32[16]{0:T(128)} %offs.3, f32[3,1,4,32,128]{4,3,2,1,0:T(8,128)} %feed.1, f32[576,35]{1,0:T(8,128)} %bitcast.3), custom_call_target="tpu_custom_call" | custom-call | tf_op jit(solution)/shard_map/relay/pallas_call | solution.py:418
  38.2 2.9 %finish.1 = (f32[2,16,32,128]{3,2,1,0:T(8,128)}, f32[1,1,4,32,128]{4,3,2,1,0:T(8,128)}) custom-call(f32[2,16,32,128]{3,2,1,0:T(8,128)} %get-tuple-element.5.partial, f32[2,4,48,128]{3,2,1,0:T(8,128)} %get-tuple-element.6.last, f32[2,4,48,128]{3,2,1,0:T(8,128)} %get-tuple-element.7.second, s32[16]{0:T(128)} %offs.3), custom_call_target="tpu_custom_call" | custom-call | tf_op jit(solution)/shard_map/finish/pallas_call | solution.py:444

commit v5 on v4

--- a/solution.py
+++ b/solution.py
@@ -31,6 +31,8 @@
     MSGS["f1", _s] = (0, _s)
     MSGS["f2", _s] = (0, _s)
     MSGS["i2", 1, _s] = (2, _s)
+    MSGS["e1", _s] = (0, _s)
+    MSGS["e2", _s] = (0, _s)
 for _l in (0, 1):
     MSGS["i1", _l, 0] = (1, 0)
     MSGS["i2", _l, 0] = (2, 0)
@@ -177,6 +179,12 @@
         V1[:, 64:96, :] = jnp.zeros((2, 32, NY), jnp.int32)
         V2[:, 48:64, :] = jnp.zeros((2, 16, NY), jnp.int32)
 
+    for end, at in ((0, 0), (strips - 1, 40)):
+        @pl.when(s == end)
+        def _(at=at):
+            for ref in (I1, I2):
+                ref[:, :, at : at + 8, :] = jnp.zeros((2, 4, 8, NY), F32)
+
     barrier = pltpu.get_barrier_semaphore()
     expected = 0
     for shift in PEERS:
@@ -214,8 +222,14 @@
     sends["v2", 1] = (rows(vel, 16, 16), rows(V2, 0, 16))
     sends["v2", -1] = (rows(vel, 0, 16), rows(V2, 48, 16))
     for layer_ in (0, 1):
-        sends["i1", layer_, 0] = (rows((Y2, Y3)[layer_], (24, 16)[layer_], 48, () if layer_ == 0 else (0,)), I1.at[layer_])
-    sends["i2", 0, 0] = (rows(Y4, 8, 48), I2.at[0])
+        sends["i1", layer_, 0] = (
+            rows((Y2, Y3)[layer_], (32, 24)[layer_], 32, () if layer_ == 0 else (0,)),
+            rows(I1, 8, 32, (layer_,)),
+        )
+    sends["i2", 0, 0] = (rows(Y4, 16, 32), rows(I2, 8, 32, (0,)))
+    for shift, at, to in ((1, 32, 0), (-1, 8, 40)):
+        sends["e1", shift] = [I1.at[:, :, pl.ds(row, 8), :] for row in (at, to)]
+        sends["e2", shift] = [rows(I2, row, 8, (0,)) for row in (at, to)]
     sends["i2", 1, 0] = (rows(Y5, 8, 32), rows(I2, 8, 32, (1,)))
     sends["i2", 1, 1] = (rows(Y5, 32, 8), rows(I2, 0, 8, (1,)))
     sends["i2", 1, -1] = (rows(Y5, 8, 8), rows(I2, 40, 8, (1,)))
@@ -356,10 +370,12 @@
     def kept(ref, count):
         return lambda j: [ref[c, j] for c in range(2 * ORDER + 2)]
 
+    received("i1")
+    start("e1")
     keep(C6, LAST[0], 0, 24)
     keep(C7, LAST[1], 1, 32)
     image([[(Y0, (), 48)], [(Y1, (0,), 40)]], True)
-    received("i1")
+    received("e1")
     image([[(I1, (0,), 8)], [(I1, (1,), 8)]], False)
     partial_out = pltpu.make_async_copy(img, img_out, lsem.at[6])
     partial_out.start()
@@ -370,17 +386,12 @@
     received("m")
     step(LAST[0], M, (), 0, kept(C6, LAST[0]), Y6, ())
     lasts_out[0].start()
+    received("i2", 0)
+    start("e2")
     step(LAST[1], Y6, (), 8, kept(C7, LAST[1]), Y7, ())
     lasts_out[1].start()
-    received("i2")
-
-    @pl.when(s == 0)
-    def _():
-        I2[1, :, 0:8, :] = jnp.zeros((4, 8, NY), F32)
-
-    @pl.when(s == strips - 1)
-    def _():
-        I2[1, :, 40:48, :] = jnp.zeros((4, 8, NY), F32)
+    received("i2", 1)
+    received("e2")
 
     second_out = pltpu.make_async_copy(I2, second, lsem.at[2])
     second_out.start()
@@ -391,7 +402,7 @@
         copy.wait()
 
     for name in copies:
-        if name[0] in ("a", "v0", "v1", "v2", "i1", "i2", "m"):
+        if name[0] in ("a", "v0", "v1", "v2", "i1", "i2", "e1", "e2", "m"):
             sent(name)
 
     @pl.when(d == depths - 1)

time: 41.3 us -> 41.2 us (level)
  the two profiles are of different devices: /device:TPU:67 before, /device:TPU:1 now
where the time goes in v5:
time: 41.2 us; the launch traced here: 40.8 us
  Pallas kernels  40.1 us (97%)
  between operations  0.64 us (2%)
    pallas_call x1, Pallas kernels, per_device(): pl.pallas_call(functools.partial(kernel, depths, strips), out_shape=(jax....  37.2 us
    pallas_call x1, Pallas kernels, per_device(): pl.pallas_call(finish, out_shape=(jax.ShapeDtypeStruct((2, noff, W, NY),...  2.89 us

profile of v5, /device:TPU:1, one launch (start us, length us, event | category | flops | bytes accessed | tf_op | source)
XLA Modules:
  0.0 40.8 jit_solution(14573869557015155637)
XLA Ops:
  0.6 37.2 %relay.1 = (f32[2,16,32,128]{3,2,1,0:T(8,128)}, f32[2,4,48,128]{3,2,1,0:T(8,128)}, f32[2,4,48,128]{3,2,1,0:T(8,128)}) custom-call(f32[1,1,4,32,128]{4,3,2,1,0:T(8,128)} %arr.1, s32[2,32,128]{2,1,0:T(8,128)} %vel.1, s32[16]{0:T(128)} %offs.3, f32[3,1,4,32,128]{4,3,2,1,0:T(8,128)} %feed.1, f32[576,35]{1,0:T(8,128)} %bitcast.3), custom_call_target="tpu_custom_call" | custom-call | tf_op jit(solution)/shard_map/relay/pallas_call | solution.py:429
  37.9 2.9 %finish.1 = (f32[2,16,32,128]{3,2,1,0:T(8,128)}, f32[1,1,4,32,128]{4,3,2,1,0:T(8,128)}) custom-call(f32[2,16,32,128]{3,2,1,0:T(8,128)} %get-tuple-element.5.partial, f32[2,4,48,128]{3,2,1,0:T(8,128)} %get-tuple-element.6.last, f32[2,4,48,128]{3,2,1,0:T(8,128)} %get-tuple-element.7.second, s32[16]{0:T(128)} %offs.3), custom_call_target="tpu_custom_call" | custom-call | tf_op jit(solution)/shard_map/finish/pallas_call | solution.py:455

commit v6 on v5

--- a/solution.py
+++ b/solution.py
@@ -37,7 +37,7 @@
     MSGS["i1", _l, 0] = (1, 0)
     MSGS["i2", _l, 0] = (2, 0)
 INDEX = {name: i for i, name in enumerate(MSGS)}
-PEERS = sorted(set(MSGS.values()))
+PEERS = sorted(set(MSGS.values()) | {(-a, -b) for a, b in MSGS.values()})
 
 
 def looked_up(nb, lev, tab, j):
@@ -137,7 +137,7 @@
         copy.wait()
 
 
-def kernel(depths, strips, arr, vel, offs, feed, table, img_out, last_out, second, img, A, V0, V1, V2, Y0, Y1, Y2, Y3, Y4, Y5, Y6, Y7, M, I1, I2, TC, TT, TW, C6, C7, ssem, rsem, lsem):
+def kernel(depths, strips, arr, vel, offs, feed, table, img_out, last_out, second, img, A, V0, V1, V2, Y0, Y1, Y2, Y3, Y4, Y5, Y6, Y7, M, I1, I2, TC, TT, TW, C6, C7, ssem, rsem, lsem, ready):
     d = lax.axis_index("depth")
     s = lax.axis_index("strip")
 
@@ -186,13 +186,27 @@
                 ref[:, :, at : at + 8, :] = jnp.zeros((2, 4, 8, NY), F32)
 
     barrier = pltpu.get_barrier_semaphore()
-    expected = 0
+    lowers, uppers = 0, 0
+    answers = []
     for shift in PEERS:
-        def greet(shift=shift):
-            pl.semaphore_signal(barrier, inc=1, device_id=peer((-shift[0], -shift[1])), device_id_type=MESH)
-
-        guarded(there(shift, -1), greet)
-        expected = expected + (1 if shift[1] == 0 else jnp.where(there(shift), 1, 0))
+        exists = there(shift)
+        if shift[1]:
+            upper, lower = (exists, None) if shift[1] > 0 else (None, exists)
+        else:
+            upper = lax.rem(d + shift[0] + depths, depths) > d
+            lower = jnp.logical_not(upper)
+        if upper is not None:
+            def greet(shift=shift):
+                pl.semaphore_signal(barrier, inc=1, device_id=peer(shift), device_id_type=MESH)
+
+            pl.when(upper)(greet)
+            uppers = uppers + jnp.where(upper, 1, 0)
+        if lower is not None:
+            def answer(shift=shift):
+                pl.semaphore_signal(ready, inc=1, device_id=peer(shift), device_id_type=MESH)
+
+            answers.append((lower, answer))
+            lowers = lowers + jnp.where(lower, 1, 0)
 
     def send(name, src, dst):
         i = INDEX[name]
@@ -261,11 +275,23 @@
     for shift, (at, count, to) in moved.items():
         entering[shift] = send(("m", shift), rows(feed, at - 8, count, (2, 0)), rows(M, to, count))
 
-    pl.semaphore_wait(barrier, expected)
-    start("v0")
-    start("a")
-    start("v1")
-    start("v2")
+    @pl.when(lowers > 0)
+    def _():
+        pl.semaphore_wait(barrier, lowers)
+
+    for lower, answer in answers:
+        pl.when(lower)(answer)
+    downward = [name for kind in ("v0", "a", "v1", "v2") for name in copies if name[0] == kind and MSGS[name][1] < 0]
+    onward = [name for kind in ("v0", "a", "v1", "v2") for name in copies if name[0] == kind and MSGS[name][1] >= 0]
+    for name in downward:
+        guarded(there(MSGS[name]), copies[name].start)
+
+    @pl.when(uppers > 0)
+    def _():
+        pl.semaphore_wait(ready, uppers)
+
+    for name in onward:
+        guarded(there(MSGS[name]), copies[name].start)
 
     @pl.when(d == depths - 1)
     def _():
@@ -448,6 +474,7 @@
                 pltpu.SemaphoreType.DMA((len(MSGS),)),
                 pltpu.SemaphoreType.DMA((len(MSGS),)),
                 pltpu.SemaphoreType.DMA((9,)),
+                pltpu.SemaphoreType.REGULAR,
             ],
             compiler_params=pltpu.CompilerParams(collective_id=0, has_side_effects=True, vmem_limit_bytes=60 * 2**20),
             name="relay",

time: 41.2 us -> 42.6 us (1.034)
  the two profiles are of different devices: /device:TPU:1 before, /device:TPU:193 now
where the time goes in v6:
time: 42.6 us; the launch traced here: 42.4 us
  Pallas kernels  41.8 us (98%)
  between operations  0.64 us (2%)
    pallas_call x1, Pallas kernels, per_device(): pl.pallas_call(functools.partial(kernel, depths, strips), out_shape=(jax....  38.9 us
    pallas_call x1, Pallas kernels, per_device(): pl.pallas_call(finish, out_shape=(jax.ShapeDtypeStruct((2, noff, W, NY),...  2.88 us

profile of v6, /device:TPU:193, one launch (start us, length us, event | category | flops | bytes accessed | tf_op | source)
XLA Modules:
  0.0 42.4 jit_solution(17401102914769069132)
XLA Ops:
  0.6 38.9 %relay.1 = (f32[2,16,32,128]{3,2,1,0:T(8,128)}, f32[2,4,48,128]{3,2,1,0:T(8,128)}, f32[2,4,48,128]{3,2,1,0:T(8,128)}) custom-call(f32[1,1,4,32,128]{4,3,2,1,0:T(8,128)} %arr.1, s32[2,32,128]{2,1,0:T(8,128)} %vel.1, s32[16]{0:T(128)} %offs.3, f32[3,1,4,32,128]{4,3,2,1,0:T(8,128)} %feed.1, f32[576,35]{1,0:T(8,128)} %bitcast.3), custom_call_target="tpu_custom_call" | custom-call | tf_op jit(solution)/shard_map/relay/pallas_call | solution.py:455
  39.6 2.9 %finish.1 = (f32[2,16,32,128]{3,2,1,0:T(8,128)}, f32[1,1,4,32,128]{4,3,2,1,0:T(8,128)}) custom-call(f32[2,16,32,128]{3,2,1,0:T(8,128)} %get-tuple-element.5.partial, f32[2,4,48,128]{3,2,1,0:T(8,128)} %get-tuple-element.6.last, f32[2,4,48,128]{3,2,1,0:T(8,128)} %get-tuple-element.7.second, s32[16]{0:T(128)} %offs.3), custom_call_target="tpu_custom_call" | custom-call | tf_op jit(solution)/shard_map/finish/pallas_call | solution.py:482

commit v7 on v5

--- a/solution.py
+++ b/solution.py
@@ -106,38 +106,23 @@
     return low[0] * high[0] + low[1] * high[1]
 
 
-def finish(partial, last, second, offs, image, outflow, out, fields, sem):
-    loads = {}
-    for row in (1, 0):
-        loads["last", row] = (last.at[row], fields.at[0, row])
+def finish(partial, last, second, offs, image, outflow, out, sem):
+    stores = [pltpu.make_async_copy(last.at[1, :, pl.ds(8, W), :], outflow.at[0, 0], sem.at[0])]
+    stores[0].start()
+    count = out.shape[1] // PARTS
     for row in (0, 1):
-        loads["second", row] = (second.at[row], fields.at[1, row])
         for part in range(PARTS):
-            some = pl.ds(part * out.shape[1] // PARTS, out.shape[1] // PARTS)
-            loads[row, part] = (partial.at[row, some], out.at[row, some])
-    loads = {name: pltpu.make_async_copy(*ends, sem.at[i]) for i, (name, ends) in enumerate(loads.items())}
-    for copy in loads.values():
-        copy.start()
-    loads["last", 1].wait()
-    stores = [pltpu.make_async_copy(fields.at[0, 1, :, pl.ds(8, W), :], outflow.at[0, 0], sem.at[len(loads)])]
-    stores[0].start()
-    loads["last", 0].wait()
-    for row in (0, 1):
-        loads["second", row].wait()
-        for part in range(PARTS):
-            loads[row, part].wait()
-            first, count = part * out.shape[1] // PARTS, out.shape[1] // PARTS
-            for k in range(first, first + count):
+            for k in range(part * count, part * count + count):
                 h = offs[k]
-                out[row, k] = out[row, k] + product(fields, (0, row), 8, h) + product(fields, (1, row), 8, h)
-            some = pl.ds(first, count)
-            stores.append(pltpu.make_async_copy(out.at[row, some], image.at[row, some], sem.at[len(loads) + len(stores)]))
+                out[row, k] = partial[row, k] + product(last, (row,), 8, h) + product(second, (row,), 8, h)
+            some = pl.ds(part * count, count)
+            stores.append(pltpu.make_async_copy(out.at[row, some], image.at[row, some], sem.at[len(stores)]))
             stores[-1].start()
     for copy in stores:
         copy.wait()
 
 
-def kernel(depths, strips, arr, vel, offs, feed, table, img_out, last_out, second, img, A, V0, V1, V2, Y0, Y1, Y2, Y3, Y4, Y5, Y6, Y7, M, I1, I2, TC, TT, TW, C6, C7, ssem, rsem, lsem):
+def kernel(depths, strips, arr, vel, offs, feed, table, img, last, second, A, V0, V1, V2, Y0, Y1, Y2, Y3, Y4, Y5, Y6, Y7, M, I1, I2, TC, TT, TW, C6, C7, ssem, rsem, lsem):
     d = lax.axis_index("depth")
     s = lax.axis_index("strip")
 
@@ -377,29 +362,17 @@
     image([[(Y0, (), 48)], [(Y1, (0,), 40)]], True)
     received("e1")
     image([[(I1, (0,), 8)], [(I1, (1,), 8)]], False)
-    partial_out = pltpu.make_async_copy(img, img_out, lsem.at[6])
-    partial_out.start()
-    lasts_out = [
-        pltpu.make_async_copy(Y6.at[:, pl.ds(16, W + 16), :], last_out.at[0], lsem.at[7]),
-        pltpu.make_async_copy(Y7.at[:, pl.ds(8, W + 16), :], last_out.at[1], lsem.at[8]),
-    ]
     received("m")
     step(LAST[0], M, (), 0, kept(C6, LAST[0]), Y6, ())
-    lasts_out[0].start()
     received("i2", 0)
     start("e2")
     step(LAST[1], Y6, (), 8, kept(C7, LAST[1]), Y7, ())
-    lasts_out[1].start()
+    last[0] = Y6[:, 16:64, :]
+    last[1] = Y7[:, 8:56, :]
     received("i2", 1)
     received("e2")
 
-    second_out = pltpu.make_async_copy(I2, second, lsem.at[2])
-    second_out.start()
-
-    partial_out.wait()
-    second_out.wait()
-    for copy in lasts_out:
-        copy.wait()
+    second[...] = I2[...]
 
     for name in copies:
         if name[0] in ("a", "v0", "v1", "v2", "i1", "i2", "e1", "e2", "m"):
@@ -421,6 +394,7 @@
 
     def per_device(arrivals, feed, velocity_index, offsets, coef_table):
         hbm = pl.BlockSpec(memory_space=pltpu.HBM)
+        vmem = pl.BlockSpec(memory_space=pltpu.VMEM)
         smem = pl.BlockSpec(memory_space=pltpu.SMEM)
         field = lambda n, *lead: pltpu.VMEM((*lead, 4, n, NY), F32)
         level = lambda n: pltpu.VMEM((2, n, NY), jnp.int32)
@@ -434,9 +408,8 @@
                 jax.ShapeDtypeStruct((2, 4, W + 16, NY), F32),
             ),
             in_specs=[hbm, hbm, smem, hbm, hbm],
-            out_specs=(hbm, hbm, hbm),
+            out_specs=(vmem, vmem, vmem),
             scratch_shapes=[
-                pltpu.VMEM((2, noff, W, NY), F32),
                 field(128), level(128), level(96), level(64),
                 field(128), field(112, 2), field(96), field(80, 2), field(64), field(48), field(80), field(64),
                 field(80), field(48, 2), field(48, 2),
@@ -449,7 +422,7 @@
                 pltpu.SemaphoreType.DMA((len(MSGS),)),
                 pltpu.SemaphoreType.DMA((9,)),
             ],
-            compiler_params=pltpu.CompilerParams(collective_id=0, has_side_effects=True, vmem_limit_bytes=60 * 2**20),
+            compiler_params=pltpu.CompilerParams(collective_id=0, has_side_effects=True, vmem_limit_bytes=40 * 2**20),
             name="relay",
         )(arrivals, velocity_index, offsets, feed, columns)
         return pl.pallas_call(
@@ -458,14 +431,13 @@
                 jax.ShapeDtypeStruct((2, noff, W, NY), F32),
                 jax.ShapeDtypeStruct((1, 1, 4, W, NY), F32),
             ),
-            in_specs=[hbm, hbm, hbm, smem],
+            in_specs=[vmem, vmem, vmem, smem],
             out_specs=(hbm, hbm),
             scratch_shapes=[
                 pltpu.VMEM((2, noff, W, NY), F32),
-                pltpu.VMEM((2, 2, 4, W + 16, NY), F32),
-                pltpu.SemaphoreType.DMA((4 * PARTS + 5,)),
+                pltpu.SemaphoreType.DMA((2 * PARTS + 1,)),
             ],
-            compiler_params=pltpu.CompilerParams(vmem_limit_bytes=60 * 2**20),
+            compiler_params=pltpu.CompilerParams(vmem_limit_bytes=8 * 2**20),
             name="finish",
         )(partial, last, second, offsets)
 

time: 41.2 us -> 43.3 us (1.051)
  local copies, waits for them, and re-layouts: 0 us -> 4.13 us
  Pallas kernels: 40.1 us -> 38 us
    unnamed x0 -> x10, local copies, waits for them, and re-layouts: none -> 4.13 us
    pallas_call x1, Pallas kernels: 2.89 us -> 1.63 us  [per_device(): pl.pallas_call(finish, out_shape=(jax.ShapeDtypeStruct((2, noff, W, NY),...]
    pallas_call x1, Pallas kernels: 37.2 us -> 36.3 us  [per_device(): pl.pallas_call(functools.partial(kernel, depths, strips), out_shape=(jax....]
where the time goes in v7:
time: 43.3 us; the launch traced here: 42.8 us
  Pallas kernels  38 us (88%)
  local copies, waits for them, and re-layouts  4.13 us (10%)
  between operations  0.65 us (2%)
    pallas_call x1, Pallas kernels, per_device(): pl.pallas_call(functools.partial(kernel, depths, strips), out_shape=(jax....  36.3 us
    unnamed x10, local copies, waits for them, and re-layouts  4.13 us
    pallas_call x1, Pallas kernels, per_device(): pl.pallas_call(finish, out_shape=(jax.ShapeDtypeStruct((2, noff, W, NY),...  1.63 us

profile of v7, /device:TPU:1, one launch (start us, length us, event | category | flops | bytes accessed | tf_op | source)
XLA Modules:
  0.0 42.8 jit_solution(16639784990030439651)
XLA Ops:
  0.6 0.0 copy-start.4
  0.6 0.6 %copy-done.4 = s32[16]{0:T(128)S(1)} copy-done((s32[16]{0:T(128)S(1)}, s32[16]{0:T(128)}, u32[]{:S(2)}) %copy-start.4) | copy-done | bytes 88
  1.3 0.0 copy-start
  1.3 1.0 %copy-done = f32[35,9,2,1,32]{0,4,3,2,1:T(8,128)S(1)} copy-done((f32[35,9,2,1,32]{0,4,3,2,1:T(8,128)S(1)}, f32[35,9,2,1,32]{0,4,3,2,1:T(8,128)}, u32[]{:S(2)}) %copy-start) | copy-done | bytes 80664
  2.2 0.0 copy-start.1
  2.3 0.9 %copy-done.1 = f32[3,1,4,32,128]{4,3,2,1,0:T(8,128)S(1)} copy-done((f32[3,1,4,32,128]{4,3,2,1,0:T(8,128)S(1)}, f32[3,1,4,32,128]{4,3,2,1,0:T(8,128)}, u32[]{:S(2)}) %copy-start.1) | copy-done | bytes 196632
  3.2 0.0 copy-start.2
  3.2 0.8 %copy-done.2 = f32[1,1,4,32,128]{4,3,2,1,0:T(8,128)S(1)} copy-done((f32[1,1,4,32,128]{4,3,2,1,0:T(8,128)S(1)}, f32[1,1,4,32,128]{4,3,2,1,0:T(8,128)}, u32[]{:S(2)}) %copy-start.2) | copy-done | bytes 65560
  4.0 0.0 copy-start.3
  4.0 0.8 %copy-done.3 = s32[2,32,128]{2,1,0:T(8,128)S(1)} copy-done((s32[2,32,128]{2,1,0:T(8,128)S(1)}, s32[2,32,128]{2,1,0:T(8,128)}, u32[]{:S(2)}) %copy-start.3) | copy-done | bytes 32792
  4.8 36.3 %relay.1 = (f32[2,16,32,128]{3,2,1,0:T(8,128)S(1)}, f32[2,4,48,128]{3,2,1,0:T(8,128)S(1)}, f32[2,4,48,128]{3,2,1,0:T(8,128)S(1)}) custom-call(f32[1,1,4,32,128]{4,3,2,1,0:T(8,128)S(1)} %copy-done.2, s32[2,32,128]{2,1,0:T(8,128)S(1)} %copy-done.3, s32[16]{0:T(128)S(1)} %copy-done.4, f32[3,1,4,32,128]{4,3,2,1,0:T(8,128)S(1)} %copy-done.1, f32[576,35]{1,0:T(8,128)S(1)} %bitcast.3), custom_call_target="tpu_custom_call" | custom-call | tf_op jit(solution)/shard_map/relay/pallas_call | solution.py:403
  41.1 1.6 %finish.1 = (f32[2,16,32,128]{3,2,1,0:T(8,128)}, f32[1,1,4,32,128]{4,3,2,1,0:T(8,128)}) custom-call(f32[2,16,32,128]{3,2,1,0:T(8,128)S(1)} %get-tuple-element.5.partial, f32[2,4,48,128]{3,2,1,0:T(8,128)S(1)} %get-tuple-element.6.last, f32[2,4,48,128]{3,2,1,0:T(8,128)S(1)} %get-tuple-element.7.second, s32[16]{0:T(128)S(1)} %copy-done.4), custom_call_target="tpu_custom_call" | custom-call | tf_op jit(solution)/shard_map/finish/pallas_call | solution.py:428
Async XLA Ops:
  0.6 0.7 %copy-start.4 = (s32[16]{0:T(128)S(1)}, s32[16]{0:T(128)}, u32[]{:S(2)}) copy-start(s32[16]{0:T(128)} %offs.3) | copy-start | bytes 196
  1.3 1.0 %copy-start = (f32[35,9,2,1,32]{0,4,3,2,1:T(8,128)S(1)}, f32[35,9,2,1,32]{0,4,3,2,1:T(8,128)}, u32[]{:S(2)}) copy-start(f32[35,9,2,1,32]{0,4,3,2,1:T(8,128)} %param.9) | copy-start | bytes 241924
  2.2 0.9 %copy-start.1 = (f32[3,1,4,32,128]{4,3,2,1,0:T(8,128)S(1)}, f32[3,1,4,32,128]{4,3,2,1,0:T(8,128)}, u32[]{:S(2)}) copy-start(f32[3,1,4,32,128]{4,3,2,1,0:T(8,128)} %feed.1) | copy-start | bytes 589828
  3.2 0.8 %copy-start.2 = (f32[1,1,4,32,128]{4,3,2,1,0:T(8,128)S(1)}, f32[1,1,4,32,128]{4,3,2,1,0:T(8,128)}, u32[]{:S(2)}) copy-start(f32[1,1,4,32,128]{4,3,2,1,0:T(8,128)} %arr.1) | copy-start | bytes 196612
  4.0 0.8 %copy-start.3 = (s32[2,32,128]{2,1,0:T(8,128)S(1)}, s32[2,32,128]{2,1,0:T(8,128)}, u32[]{:S(2)}) copy-start(s32[2,32,128]{2,1,0:T(8,128)} %vel.1) | copy-start | bytes 98308
